TPU v7x, 256 devices: a whole 4x4x8 slice. The times are simulated.
256 devices in a mesh: inner: 4 (over x_hi, core), outer: 64 (over y, x_lo, z).
Axes of the slice: x: 4 (x_hi: 2, x_lo: 2; x = x_hi * 2 + x_lo), y: 4, z: 8, core: 2. Of those that a mesh axis runs over, the one named last changes fastest.
Arguments:
- queries: bfloat16 [65536, 512], P(('inner', 'outer')), may hold values from -12 to 12
- keys: bfloat16 [65536, 128], P(('inner', 'outer')), may hold values from -12 to 12
- values: bfloat16 [65536, 128], P(('inner', 'outer')), may hold values from -6 to 6
- out_grad: bfloat16 [65536, 512], P(('inner', 'outer')), may hold values from -6 to 6
- block_place: int32 [512], replicated, may hold values from 0 to 511, each once
Outputs:
- query_grad: bfloat16 [65536, 512], P(('inner', 'outer'))
- key_grad: bfloat16 [65536, 128], P(('inner', 'outer'))
- value_grad: bfloat16 [65536, 128], P(('inner', 'outer'))
Inputs may be any that keep to these rules, and one draw needn't show every extreme that they name: `block_place`: every block place appears exactly once.
All inputs are finite; a program needn't handle non-finite values.
Results may differ from a plain program's by a relative error of at most 0.017.
Values may be sent and summed in bfloat16 or wider, within the bound.
A program may use at most 128 MiB of HBM per device.

v0:
```python
import math

import jax
import jax.numpy as jnp
from jax import lax
from jax.sharding import PartitionSpec as P

STEPS = 4


def sent_together(arrays, axis, dim, along):
    widths = [a.shape[along] for a in arrays]
    both = jnp.concatenate(arrays, axis=along)
    result = lax.all_gather(both, axis, axis=dim, tiled=True)
    return tuple(jnp.split(result, [sum(widths[:k]) for k in range(1, len(widths))], axis=along))


def as_sent(array):

    def short(part):
        return part.astype(jnp.bfloat16) if part.dtype == jnp.float32 else part

    return jax.tree.map(short, array)


def from_behind(block, axis, distance):
    devices = range(lax.axis_size(axis))
    route = [((i - distance) % len(devices), i) for i in devices]
    return lax.ppermute(block, axis, route)


def cut_along(array, dim, devices):
    dims = array.shape
    pieces = array.reshape(*dims[:dim], devices, dims[dim] // devices, *dims[dim + 1 :])
    return jnp.moveaxis(pieces, dim, 0)


def summed_on_arrival(array, axis, dim):
    devices = lax.axis_size(axis)
    pieces = lax.all_to_all(cut_along(array, dim, devices), axis, 0, 0, tiled=True)
    return jnp.sum(pieces.astype(jnp.float32), axis=0)


def in_one_piece(arrays, axis, dim, along):
    ends, at = ([], 0)
    for a in arrays[:-1]:
        at += a.shape[along]
        ends.append(at)
    both = jnp.concatenate(arrays, axis=along)
    return tuple(jnp.split(summed_on_arrival(both, axis, dim), ends, axis=along))


def per_device(queries, keys, values, out_grad, block_place):
    row_count = keys.shape[0]
    head_size = keys.shape[1]
    head_count = queries.shape[1] // head_size
    inner_size = lax.axis_size("inner")
    outer_size = lax.axis_size("outer")
    block_len = row_count // 2
    group_rows = inner_size * row_count
    score_scale = 1.0 / math.sqrt(head_size)
    inner_index = lax.axis_index("inner")
    outer_index = lax.axis_index("outer")
    places = block_place.reshape(inner_size, outer_size, 2)
    offsets = jnp.arange(block_len, dtype=jnp.int32)
    own_blocks = lax.dynamic_index_in_dim(
        lax.dynamic_index_in_dim(places, inner_index, 0, False), outer_index, 0, False
    )
    query_place = (own_blocks[:, None] * block_len + offsets[None, :]).reshape(row_count)
    query_rows = queries.reshape(row_count, head_count, head_size)
    grad_rows = out_grad.reshape(row_count, head_count, head_size)
    group_keys, group_values = sent_together((keys, values), "inner", 0, 1)
    bundles = [(group_keys, group_values)]
    for step in range(1, STEPS):
        bundles.append(from_behind(as_sent(bundles[-1]), "outer", 1))
    masks = []
    score_list = []
    run_max = jnp.full((row_count, head_count), -1e30, jnp.float32)
    for step in range(STEPS):
        key_rows = bundles[step][0]
        scores = (
            jnp.einsum("thd,kd->thk", query_rows, key_rows, preferred_element_type=jnp.float32)
            * score_scale
        )
        source = (outer_index - step) % outer_size
        bundle_blocks = lax.dynamic_index_in_dim(places, source, 1, False)
        allowed = (bundle_blocks[:, :, None] * block_len + offsets).reshape(group_rows)[
            None, None, :
        ] <= query_place[:, None, None]
        scores = jnp.where(allowed, scores, -1e30)
        run_max = jnp.maximum(run_max, jnp.max(scores, axis=-1))
        masks.append(allowed)
        score_list.append(scores)
    run_sum = jnp.zeros((row_count, head_count), jnp.float32)
    for step in range(STEPS):
        run_sum = run_sum + jnp.sum(
            jnp.where(masks[step], jnp.exp(score_list[step] - run_max[..., None]), 0.0), axis=-1
        )
    log_total = run_max + jnp.log(run_sum)
    prob_list = []
    grad_prob_list = []
    row_dot = jnp.zeros((row_count, head_count), jnp.float32)
    for step in range(STEPS):
        value_rows = bundles[step][1]
        probs = jnp.where(masks[step], jnp.exp(score_list[step] - log_total[..., None]), 0.0)
        probs_low = probs.astype(jnp.bfloat16)
        grad_probs = jnp.einsum(
            "thd,kd->thk", grad_rows, value_rows, preferred_element_type=jnp.float32
        )
        row_dot = row_dot + jnp.sum(probs_low.astype(jnp.float32) * grad_probs, axis=-1)
        prob_list.append(probs)
        grad_prob_list.append(grad_probs)
    query_acc = jnp.zeros((row_count, head_count, head_size), jnp.float32)
    key_sum = jnp.zeros((group_rows, head_size), jnp.float32)
    value_sum = jnp.zeros((group_rows, head_size), jnp.float32)
    for step in reversed(range(STEPS)):
        bundle_key_rows = bundles[step][0]
        bundle_probs = prob_list[step]
        bundle_probs_low = bundle_probs.astype(jnp.bfloat16)
        grad_scores = (bundle_probs * (grad_prob_list[step] - row_dot[..., None])).astype(
            jnp.bfloat16
        )
        query_part = jnp.einsum(
            "thk,kd->thd", grad_scores, bundle_key_rows, preferred_element_type=jnp.float32
        )
        key_part = (
            jnp.einsum("thk,thd->kd", grad_scores, query_rows, preferred_element_type=jnp.float32)
            * score_scale
        )
        value_part = jnp.einsum(
            "thk,thd->kd", bundle_probs_low, grad_rows, preferred_element_type=jnp.float32
        )
        query_part, key_part, value_part = (query_part, key_part, value_part)
        query_acc = query_acc + query_part
        key_sum = key_sum + key_part
        value_sum = value_sum + value_part
        if step > 0:
            key_sum, value_sum = (
                from_behind(key_sum.astype(jnp.bfloat16), "outer", -1).astype(key_sum.dtype),
                from_behind(value_sum.astype(jnp.bfloat16), "outer", -1).astype(value_sum.dtype),
            )
    key_total, value_total = in_one_piece(
        (key_sum.astype(jnp.bfloat16), value_sum.astype(jnp.bfloat16)), "inner", 0, 1
    )
    query_grad = (
        (query_acc * score_scale).reshape(row_count, head_count * head_size).astype(jnp.bfloat16)
    )
    return (query_grad, key_total.astype(jnp.bfloat16), value_total.astype(jnp.bfloat16))


def solution(mesh):
    placed = (
        P(("inner", "outer"), None),
        P(("inner", "outer"), None),
        P(("inner", "outer"), None),
        P(("inner", "outer"), None),
        P(),
    )
    return jax.shard_map(
        per_device,
        mesh=mesh,
        in_specs=placed,
        out_specs=(
            P(("inner", "outer"), None),
            P(("inner", "outer"), None),
            P(("inner", "outer"), None),
        ),
        check_vma=False,
    )
```

profile of v0, /device:TPU:1, one launch (start us, length us, event | category | flops | bytes accessed | tf_op | source)
XLA Modules:
  0.0 144.5 jit_solution(15121531542719372215)
XLA Ops:
  1.5 11.1 %all_gather.3 = bf16[1024,256]{1,0:T(8,128)(2,1)S(1)} all-gather(bf16[256,256]{1,0:T(8,128)(2,1)S(1)} %pad_maximum_fusion.1), channel_id=1, replica_groups=mesh['inner'=4,'outer'=64] {'inner'}, dimensions={0}, use_global_device_ids=true | all-gather | bytes 655360 | tf_op jit(solution)/shard_map/all_gather | solution.py:14
  13.3 1.6 %collective-permute-start.3 = (bf16[1024,128]{1,0:T(8,128)(2,1)S(1)}, bf16[1024,128]{1,0:T(8,128)(2,1)S(1)}, u32[]{:S(2)}, u32[]{:S(2)}) collective-permute-start(bf16[1024,128]{1,0:T(8,128)(2,1)S(1)} %get-tuple-element.21), channel_id=1, source_target_pairs={{63,0},{0,1},{1,2},{2,3},{3,4},{4,5},{5,6},{6,7},{7,8},{8,9},{9,10... | collective-permute-start | bytes 786440 | tf_op jit(solution)/shard_map/ppermute | solution.py:29
  17.0 1.1 copy.137
  20.9 2.6 %fusion.34 = f32[1024,256,4]{1,0,2:T(8,128)} fusion(bf16[256,4,128]{0,2,1:T(8,128)(2,1)S(1)} %bitcast.220, bf16[1024,256]{1,0:T(8,128)(2,1)S(1)} %all_gather.3), kind=kOutput, calls=%fused_computation.74 | convolution fusion | flops 268435456 | bytes 4718592 | tf_op jit(solution)/shard_map/thd,kd->thk/dot_general | solution.py:107
  23.6 3.2 %collective-permute-done = bf16[1024,128]{1,0:T(8,128)(2,1)S(1)} collective-permute-done((bf16[1024,128]{1,0:T(8,128)(2,1)S(1)}, bf16[1024,128]{1,0:T(8,128)(2,1)S(1)}, u32[]{:S(2)}, u32[]{:S(2)}) %collective-permute-start) | collective-permute-done | bytes 262176 | tf_op jit(solution)/shard_map/ppermute | solution.py:29
  26.7 5.6 %collective-permute-done.3 = bf16[1024,128]{1,0:T(8,128)(2,1)S(1)} collective-permute-done((bf16[1024,128]{1,0:T(8,128)(2,1)S(1)}, bf16[1024,128]{1,0:T(8,128)(2,1)S(1)}, u32[]{:S(2)}, u32[]{:S(2)}) %collective-permute-start.3) | collective-permute-done | bytes 262176 | tf_op jit(solution)/shard_map/ppermute | solution.py:29
  33.2 4.5 %collective-permute-done.1 = bf16[1024,128]{1,0:T(8,128)(2,1)S(1)} collective-permute-done((bf16[1024,128]{1,0:T(8,128)(2,1)S(1)}, bf16[1024,128]{1,0:T(8,128)(2,1)S(1)}, u32[]{:S(2)}, u32[]{:S(2)}) %collective-permute-start.1) | collective-permute-done | bytes 262176 | tf_op jit(solution)/shard_map/ppermute | solution.py:29
  37.7 6.0 %collective-permute-done.4 = bf16[1024,128]{1,0:T(8,128)(2,1)S(1)} collective-permute-done((bf16[1024,128]{1,0:T(8,128)(2,1)S(1)}, bf16[1024,128]{1,0:T(8,128)(2,1)S(1)}, u32[]{:S(2)}, u32[]{:S(2)}) %collective-permute-start.4) | collective-permute-done | bytes 262176 | tf_op jit(solution)/shard_map/ppermute | solution.py:29
  44.5 2.7 %fusion.30 = f32[1024,256,4]{1,0,2:T(8,128)} fusion(bf16[256,4,128]{0,2,1:T(8,128)(2,1)S(1)} %bitcast.221, bf16[1024,128]{1,0:T(8,128)(2,1)S(1)} %collective-permute-done.4), kind=kOutput, calls=%fused_computation.70 | convolution fusion | flops 268435456 | bytes 4718592 | tf_op jit(solution)/shard_map/thd,kd->thk/dot_general | solution.py:107
  47.2 1.1 collective-permute-done.2
  49.1 4.3 %select_reduce_fusion.2 = (f32[256,4]{0,1:T(4,128)S(1)}, f32[256,4]{0,1:T(4,128)S(1)}, f32[256,4]{0,1:T(4,128)S(1)}, f32[256,4]{0,1:T(4,128)S(1)}) fusion(f32[1024,256,4]{1,0,2:T(8,128)S(1)} %get-tuple-element.41, f32[256,4]{0,1:T(4,128)S(1)} %maximum_maximum_fusion, pred[256,1024]{0,1:T(8,128)(4,1)S(1)} %get-tuple-element.33, ...), kind=kLoop, calls=%fused_computation.30 | loop fusion | flops 20967424 | bytes 17846272 | tf_op jit(solution)/shard_map/reduce_sum | solution.py:96
  53.5 2.0 %fusion.27 = bf16[1024,128]{1,0:T(8,128)(2,1)} fusion(bf16[256,4,128]{0,2,1:T(8,128)(2,1)S(1)} %bitcast.222, f32[1024,256,4]{1,0,2:T(8,128)S(1)} %get-tuple-element.37, f32[256,4]{0,1:T(4,128)S(1)} %log_add_fusion, pred[256,1024]{0,1:T(8,128)(4,1)S(1)} %get-tuple-element.35), kind=kOutput, calls=%fused_computation.56 | convolution fusion | flops 273809408 | bytes 4984832 | tf_op jit(solution)/shard_map/thk,thd->kd/dot_general | solution.py:130
  55.4 2.1 %convolution_bitcast_fusion = f32[1024,128]{1,0:T(8,128)} fusion(bf16[256,4,128]{0,2,1:T(8,128)(2,1)S(1)} %bitcast.223, f32[1024,256,4]{1,0,2:T(8,128)S(1)} %get-tuple-element.43, f32[256,4]{0,1:T(4,128)S(1)} %log_add_fusion, pred[256,1024]{0,1:T(8,128)(4,1)S(1)} %get-tuple-element.32), kind=kOutput, calls=%fused_computation.40 | convolution fusion | flops 273678336 | bytes 5246976 | tf_op jit(solution)/shard_map/thk,thd->kd/dot_general | solution.py:130
  57.5 4.6 %collective-permute-start.9 = (bf16[1024,128]{1,0:T(8,128)(2,1)}, bf16[1024,128]{1,0:T(8,128)(2,1)}, u32[]{:S(2)}, u32[]{:S(2)}) collective-permute-start(bf16[1024,128]{1,0:T(8,128)(2,1)} %fusion.27), channel_id=1, source_target_pairs={{1,0},{2,1},{3,2},{4,3},{5,4},{6,5},{7,6},{8,7},{9,8},{10,9},{11,1... | collective-permute-start | bytes 786440 | tf_op jit(solution)/shard_map/ppermute | solution.py:29
  62.1 2.1 %convolution_bitcast_fusion.1 = f32[1024,128]{1,0:T(8,128)} fusion(bf16[256,4,128]{0,2,1:T(8,128)(2,1)S(1)} %bitcast.224, f32[1024,256,4]{1,0,2:T(8,128)S(1)} %get-tuple-element.41, f32[256,4]{0,1:T(4,128)S(1)} %log_add_fusion, pred[256,1024]{0,1:T(8,128)(4,1)S(1)} %get-tuple-element.33), kind=kOutput, calls=%fused_computation.41 | convolution fusion | flops 273678336 | bytes 5246976 | tf_op jit(solution)/shard_map/thk,thd->kd/dot_general | solution.py:130
  64.2 2.6 %fusion.36 = f32[1024,256,4]{1,0,2:T(8,128)} fusion(bf16[256,4,128]{0,2,1:T(8,128)(2,1)S(1)} %bitcast.225, bf16[1024,128]{1,0:T(8,128)(2,1)S(1)} %collective-permute-done.5), kind=kOutput, calls=%fused_computation.76 | convolution fusion | flops 268435456 | bytes 4718592 | tf_op jit(solution)/shard_map/thd,kd->thk/dot_general | solution.py:107
  66.9 9.6 %fusion.3 = (f32[256,4]{0,1:T(4,128)S(1)}, f32[256,4]{0,1:T(4,128)S(1)}, f32[256,4]{0,1:T(4,128)S(1)}, f32[256,4]{0,1:T(4,128)S(1)}, f32[1024,256,4]{1,0,2:T(8,128)}) fusion(f32[256,4]{0,1:T(4,128)S(1)} %log_add_fusion, f32[1024,256,4]{1,0,2:T(8,128)S(1)} %get-tuple-element.41, pred[256,1024]{0,1:T(8,128)(4,1)S(1)} %get-tuple-element.33, ...), kind=kOutput, calls=%fused_computation.7 | convolution fusion | flops 301985792 | bytes 35147776 | tf_op jit(solution)/shard_map/thd,kd->thk/dot_general | solution.py:107
  76.4 14.0 %fusion.11 = (bf16[256,4,1024]{0,2,1:T(8,128)(2,1)}, bf16[256,4,1024]{0,2,1:T(8,128)(2,1)}, bf16[256,4,1024]{0,2,1:T(8,128)(2,1)}, bf16[256,4,1024]{0,2,1:T(8,128)(2,1)}) fusion(f32[1024,256,4]{1,0,2:T(8,128)} %fusion.36, f32[1024,256,4]{1,0,2:T(8,128)} %copy-done.1, f32[256,4]{0,1:T(4,128)S(1)} %add_add_fusion, f32[256,4]{0,1:T(4,128)S(1)} %log_add_fusion, ...), kind=kLoop, calls=%fused_computation.19 | loop fusion | flops 29360128 | bytes 42999808 | tf_op jit(solution)/shard_map/convert_element_type | solution.py:120
  90.4 3.0 %fusion.46 = f32[256,4,128]{0,2,1:T(8,128)} fusion(bf16[256,4,1024]{0,2,1:T(8,128)(2,1)} %get-tuple-element.31, bf16[1024,256]{1,0:T(8,128)(2,1)S(1)} %all_gather.3), kind=kOutput, calls=%fused_computation.86 | convolution fusion | flops 268435456 | bytes 2883584 | tf_op jit(solution)/shard_map/thk,kd->thd/dot_general | solution.py:123
  93.5 2.3 %fusion.29 = bf16[1024,128]{1,0:T(8,128)(2,1)S(1)} fusion(bf16[256,4,1024]{0,2,1:T(8,128)(2,1)} %get-tuple-element.28, bf16[256,4,128]{0,2,1:T(8,128)(2,1)S(1)} %bitcast.216), kind=kOutput, calls=%fused_computation.58 | convolution fusion | flops 268697600 | bytes 2621440 | tf_op jit(solution)/shard_map/thk,thd->kd/dot_general | solution.py:127
  96.6 2.4 %add_convert_fusion.2 = bf16[1024,128]{1,0:T(8,128)(2,1)S(1)} fusion(bf16[1024,128]{1,0:T(8,128)(2,1)} %collective-permute-done.9, bf16[256,4,128]{0,2,1:T(8,128)(2,1)S(1)} %bitcast.227, f32[1024,256,4]{1,0,2:T(8,128)S(1)} %get-tuple-element.39, f32[256,4]{0,1:T(4,128)S(1)} %log_add_fusion, pred[256,1024]{0,1:T(8,128)(4,1)S(1)} %get-tuple-element.34), kind=kOutput, calls=%fused_computation.62 | convolution fusion | flops 274071552 | bytes 5246976 | tf_op jit(solution)/shard_map/thk,thd->kd/dot_general | solution.py:130
  99.4 1.7 %collective-permute-done.6 = bf16[1024,128]{1,0:T(8,128)(2,1)S(1)} collective-permute-done((bf16[1024,128]{1,0:T(8,128)(2,1)S(1)}, bf16[1024,128]{1,0:T(8,128)(2,1)S(1)}, u32[]{:S(2)}, u32[]{:S(2)}) %collective-permute-start.6) | collective-permute-done | bytes 262176 | tf_op jit(solution)/shard_map/ppermute | solution.py:29
  101.8 4.8 %collective-permute-start.7 = (bf16[1024,128]{1,0:T(8,128)(2,1)S(1)}, bf16[1024,128]{1,0:T(8,128)(2,1)S(1)}, u32[]{:S(2)}, u32[]{:S(2)}) collective-permute-start(bf16[1024,128]{1,0:T(8,128)(2,1)S(1)} %add_convert_fusion.5), channel_id=1, source_target_pairs={{1,0},{2,1},{3,2},{4,3},{5,4},{6,5},{7,6},{8,7},{9,8},{10,9},{11,1... | collective-permute-start | bytes 786440 | tf_op jit(solution)/shard_map/ppermute | solution.py:29
  107.7 4.3 %collective-permute-start.11 = (bf16[1024,128]{1,0:T(8,128)(2,1)S(1)}, bf16[1024,128]{1,0:T(8,128)(2,1)S(1)}, u32[]{:S(2)}, u32[]{:S(2)}) collective-permute-start(bf16[1024,128]{1,0:T(8,128)(2,1)S(1)} %add_convert_fusion.1), channel_id=1, source_target_pairs={{1,0},{2,1},{3,2},{4,3},{5,4},{6,5},{7,6},{8,7},{9,8},{10,9},{11,1... | collective-permute-start | bytes 786440 | tf_op jit(solution)/shard_map/ppermute | solution.py:29
  112.1 1.2 collective-permute-done.7
  113.3 3.3 %collective-permute-start.8 = (bf16[1024,128]{1,0:T(8,128)(2,1)S(1)}, bf16[1024,128]{1,0:T(8,128)(2,1)S(1)}, u32[]{:S(2)}, u32[]{:S(2)}) collective-permute-start(bf16[1024,128]{1,0:T(8,128)(2,1)S(1)} %add_convert_fusion.4), channel_id=1, source_target_pairs={{1,0},{2,1},{3,2},{4,3},{5,4},{6,5},{7,6},{8,7},{9,8},{10,9},{11,1... | collective-permute-start | bytes 786440 | tf_op jit(solution)/shard_map/ppermute | solution.py:29
  116.7 1.3 fusion.38
  119.0 5.6 %collective-permute-done.8 = bf16[1024,128]{1,0:T(8,128)(2,1)S(1)} collective-permute-done((bf16[1024,128]{1,0:T(8,128)(2,1)S(1)}, bf16[1024,128]{1,0:T(8,128)(2,1)S(1)}, u32[]{:S(2)}, u32[]{:S(2)}) %collective-permute-start.8) | collective-permute-done | bytes 262176 | tf_op jit(solution)/shard_map/ppermute | solution.py:29
  125.4 8.9 %all-to-all-start = ((bf16[4,256,256]{2,1,0:T(8,128)(2,1)}), bf16[4,256,256]{2,1,0:T(8,128)(2,1)S(1)}, u32[]{:S(2)}, u32[]{:S(2)}) async-start(bf16[4,256,256]{2,1,0:T(8,128)(2,1)} %bitcast.39), calls=%async_computation | async-start | bytes 1048576 | tf_op jit(solution)/shard_map/all_to_all | solution.py:40
  134.3 1.4 fusion.42
  135.8 2.3 %fusion.28 = bf16[256,4,128]{0,2,1:T(8,128)(2,1)S(1)} fusion(f32[256,4,128]{0,2,1:T(8,128)S(1)} %copy-done.11, f32[256,4,128]{0,2,1:T(8,128)S(1)} %fusion.42, f32[256,4,128]{0,2,1:T(8,128)} %fusion.38, bf16[256,4,1024]{0,2,1:T(8,128)(2,1)} %get-tuple-element.28, bf16[1024,128]{1,0:T(8,128)(2,1)} %copy-done.12), kind=kOutput, calls=%fused_computation.57 | convolution fusion | flops 269090816 | bytes 4194304 | tf_op jit(solution)/shard_map/thk,kd->thd/dot_general | solution.py:123
  138.9 4.9 %all-to-all-done = bf16[4,256,256]{2,1,0:T(8,128)(2,1)S(1)} async-done(((bf16[4,256,256]{2,1,0:T(8,128)(2,1)}), bf16[4,256,256]{2,1,0:T(8,128)(2,1)S(1)}, u32[]{:S(2)}, u32[]{:S(2)}) %all-to-all-start) | async-done | bytes 524320 | tf_op jit(solution)/shard_map/all_to_all | solution.py:40
  (93 shorter events, 15.4 us)
Async XLA Ops:
  12.7 14.1 %collective-permute-start = (bf16[1024,128]{1,0:T(8,128)(2,1)S(1)}, bf16[1024,128]{1,0:T(8,128)(2,1)S(1)}, u32[]{:S(2)}, u32[]{:S(2)}) collective-permute-start(bf16[1024,128]{1,0:T(8,128)(2,1)S(1)} %get-tuple-element.20), channel_id=1, source_target_pairs={{63,0},{0,1},{1,2},{2,3},{3,4},{4,5},{5,6},{6,7},{7,8},{8,9},{9,10... | collective-permute-start | bytes 786440 | tf_op jit(solution)/shard_map/ppermute | solution.py:29
  13.3 19.0 %collective-permute-start.3 = (bf16[1024,128]{1,0:T(8,128)(2,1)S(1)}, bf16[1024,128]{1,0:T(8,128)(2,1)S(1)}, u32[]{:S(2)}, u32[]{:S(2)}) collective-permute-start(bf16[1024,128]{1,0:T(8,128)(2,1)S(1)} %get-tuple-element.21), channel_id=1, source_target_pairs={{63,0},{0,1},{1,2},{2,3},{3,4},{4,5},{5,6},{6,7},{7,8},{8,9},{9,10... | collective-permute-start | bytes 786440 | tf_op jit(solution)/shard_map/ppermute | solution.py:29
  19.2 4.4 %copy-start.8 = (bf16[256,512]{0,1:T(8,128)(2,1)}, bf16[256,512]{0,1:T(8,128)(2,1)S(1)}, u32[]{:S(2)}) copy-start(bf16[256,512]{0,1:T(8,128)(2,1)S(1)} %copy.138) | copy-start | bytes 786436
  20.1 46.7 %copy-start.6 = (pred[256,1024]{0,1:T(8,128)(4,1)}, pred[256,1024]{0,1:T(8,128)(4,1)S(1)}, u32[]{:S(2)}) copy-start(pred[256,1024]{0,1:T(8,128)(4,1)S(1)} %get-tuple-element.33) | copy-start | bytes 786436
  20.1 46.7 %copy-start.7 = (pred[256,1024]{0,1:T(8,128)(4,1)}, pred[256,1024]{0,1:T(8,128)(4,1)S(1)}, u32[]{:S(2)}) copy-start(pred[256,1024]{0,1:T(8,128)(4,1)S(1)} %get-tuple-element.35) | copy-start | bytes 786436
  26.7 16.9 %copy-start.13 = (bf16[1024,128]{1,0:T(8,128)(2,1)}, bf16[1024,128]{1,0:T(8,128)(2,1)S(1)}, u32[]{:S(2)}) copy-start(bf16[1024,128]{1,0:T(8,128)(2,1)S(1)} %collective-permute-done) | copy-start | bytes 786436
  26.7 10.9 %collective-permute-start.1 = (bf16[1024,128]{1,0:T(8,128)(2,1)S(1)}, bf16[1024,128]{1,0:T(8,128)(2,1)S(1)}, u32[]{:S(2)}, u32[]{:S(2)}) collective-permute-start(bf16[1024,128]{1,0:T(8,128)(2,1)S(1)} %collective-permute-done), channel_id=1, source_target_pairs={{63,0},{0,1},{1,2},{2,3},{3,4},{4,5},{5,6},{6,7},{7,8},{8,9},{9,10... | collective-permute-start | bytes 786440 | tf_op jit(solution)/shard_map/ppermute | solution.py:29
  32.4 11.3 %copy-start.18 = (bf16[1024,128]{1,0:T(8,128)(2,1)}, bf16[1024,128]{1,0:T(8,128)(2,1)S(1)}, u32[]{:S(2)}) copy-start(bf16[1024,128]{1,0:T(8,128)(2,1)S(1)} %collective-permute-done.3) | copy-start | bytes 786436
  32.4 11.3 %collective-permute-start.4 = (bf16[1024,128]{1,0:T(8,128)(2,1)S(1)}, bf16[1024,128]{1,0:T(8,128)(2,1)S(1)}, u32[]{:S(2)}, u32[]{:S(2)}) collective-permute-start(bf16[1024,128]{1,0:T(8,128)(2,1)S(1)} %collective-permute-done.3), channel_id=1, source_target_pairs={{63,0},{0,1},{1,2},{2,3},{3,4},{4,5},{5,6},{6,7},{7,8},{8,9},{9,10... | collective-permute-start | bytes 786440 | tf_op jit(solution)/shard_map/ppermute | solution.py:29
  32.4 12.1 %copy-start.9 = (bf16[256,512]{0,1:T(8,128)(2,1)S(1)}, bf16[256,512]{0,1:T(8,128)(2,1)}, u32[]{:S(2)}) copy-start(bf16[256,512]{0,1:T(8,128)(2,1)} %copy-done.8) | copy-start | bytes 786436
  33.2 33.7 %copy-start = (f32[1024,256,4]{1,0,2:T(8,128)}, f32[1024,256,4]{1,0,2:T(8,128)S(1)}, u32[]{:S(2)}) copy-start(f32[1024,256,4]{1,0,2:T(8,128)S(1)} %get-tuple-element.41) | copy-start | bytes 12582916
  37.7 9.5 %copy-start.14 = (bf16[1024,128]{1,0:T(8,128)(2,1)}, bf16[1024,128]{1,0:T(8,128)(2,1)S(1)}, u32[]{:S(2)}) copy-start(bf16[1024,128]{1,0:T(8,128)(2,1)S(1)} %collective-permute-done.1) | copy-start | bytes 786436
  37.7 10.6 %collective-permute-start.2 = (bf16[1024,128]{1,0:T(8,128)(2,1)S(1)}, bf16[1024,128]{1,0:T(8,128)(2,1)S(1)}, u32[]{:S(2)}, u32[]{:S(2)}) collective-permute-start(bf16[1024,128]{1,0:T(8,128)(2,1)S(1)} %collective-permute-done.1), channel_id=1, source_target_pairs={{63,0},{0,1},{1,2},{2,3},{3,4},{4,5},{5,6},{6,7},{7,8},{8,9},{9,10... | collective-permute-start | bytes 786440 | tf_op jit(solution)/shard_map/ppermute | solution.py:29
  43.7 20.5 %collective-permute-start.5 = (bf16[1024,128]{1,0:T(8,128)(2,1)S(1)}, bf16[1024,128]{1,0:T(8,128)(2,1)S(1)}, u32[]{:S(2)}, u32[]{:S(2)}) collective-permute-start(bf16[1024,128]{1,0:T(8,128)(2,1)S(1)} %collective-permute-done.4), channel_id=1, source_target_pairs={{63,0},{0,1},{1,2},{2,3},{3,4},{4,5},{5,6},{6,7},{7,8},{8,9},{9,10... | collective-permute-start | bytes 786440 | tf_op jit(solution)/shard_map/ppermute | solution.py:29
  48.3 5.1 %copy-start.12 = (bf16[1024,128]{1,0:T(8,128)(2,1)}, bf16[1024,128]{1,0:T(8,128)(2,1)S(1)}, u32[]{:S(2)}) copy-start(bf16[1024,128]{1,0:T(8,128)(2,1)S(1)} %collective-permute-done.2) | copy-start | bytes 786436
  49.1 17.8 %copy-start.1 = (f32[1024,256,4]{1,0,2:T(8,128)}, f32[1024,256,4]{1,0,2:T(8,128)S(1)}, u32[]{:S(2)}) copy-start(f32[1024,256,4]{1,0,2:T(8,128)S(1)} %get-tuple-element.37) | copy-start | bytes 12582916
  57.5 39.1 %collective-permute-start.9 = (bf16[1024,128]{1,0:T(8,128)(2,1)}, bf16[1024,128]{1,0:T(8,128)(2,1)}, u32[]{:S(2)}, u32[]{:S(2)}) collective-permute-start(bf16[1024,128]{1,0:T(8,128)(2,1)} %fusion.27), channel_id=1, source_target_pairs={{1,0},{2,1},{3,2},{4,3},{5,4},{6,5},{7,6},{8,7},{9,8},{10,9},{11,1... | collective-permute-start | bytes 786440 | tf_op jit(solution)/shard_map/ppermute | solution.py:29
  90.4 5.4 %copy-start.4 = (bf16[256,4,1024]{0,2,1:T(8,128)(2,1)S(1)}, bf16[256,4,1024]{0,2,1:T(8,128)(2,1)}, u32[]{:S(2)}) copy-start(bf16[256,4,1024]{0,2,1:T(8,128)(2,1)} %get-tuple-element.31) | copy-start | bytes 6291460
  90.4 6.2 %copy-start.10 = (bf16[256,512]{0,1:T(8,128)(2,1)S(1)}, bf16[256,512]{0,1:T(8,128)(2,1)}, u32[]{:S(2)}) copy-start(bf16[256,512]{0,1:T(8,128)(2,1)} %copy-done.8) | copy-start | bytes 786436
  95.8 5.3 %collective-permute-start.6 = (bf16[1024,128]{1,0:T(8,128)(2,1)S(1)}, bf16[1024,128]{1,0:T(8,128)(2,1)S(1)}, u32[]{:S(2)}, u32[]{:S(2)}) collective-permute-start(bf16[1024,128]{1,0:T(8,128)(2,1)S(1)} %fusion.29), channel_id=1, source_target_pairs={{1,0},{2,1},{3,2},{4,3},{5,4},{6,5},{7,6},{8,7},{9,8},{10,9},{11,1... | collective-permute-start | bytes 786440 | tf_op jit(solution)/shard_map/ppermute | solution.py:29
  96.6 4.5 %copy-start.5 = (bf16[256,4,1024]{0,2,1:T(8,128)(2,1)S(1)}, bf16[256,4,1024]{0,2,1:T(8,128)(2,1)}, u32[]{:S(2)}) copy-start(bf16[256,4,1024]{0,2,1:T(8,128)(2,1)} %get-tuple-element.29) | copy-start | bytes 6291460
  96.6 10.0 %copy-start.2 = (bf16[256,4,1024]{0,2,1:T(8,128)(2,1)S(1)}, bf16[256,4,1024]{0,2,1:T(8,128)(2,1)}, u32[]{:S(2)}) copy-start(bf16[256,4,1024]{0,2,1:T(8,128)(2,1)} %get-tuple-element.30) | copy-start | bytes 6291460
  99.0 8.6 %copy-start.17 = (f32[1024,128]{1,0:T(8,128)S(1)}, f32[1024,128]{1,0:T(8,128)}, u32[]{:S(2)}) copy-start(f32[1024,128]{1,0:T(8,128)} %convolution_bitcast_fusion.1) | copy-start | bytes 1572868
  99.0 17.6 %copy-start.15 = (bf16[1024,128]{1,0:T(8,128)(2,1)S(1)}, bf16[1024,128]{1,0:T(8,128)(2,1)}, u32[]{:S(2)}) copy-start(bf16[1024,128]{1,0:T(8,128)(2,1)} %copy-done.14) | copy-start | bytes 786436
  99.0 8.6 %collective-permute-start.10 = (bf16[1024,128]{1,0:T(8,128)(2,1)S(1)}, bf16[1024,128]{1,0:T(8,128)(2,1)S(1)}, u32[]{:S(2)}, u32[]{:S(2)}) collective-permute-start(bf16[1024,128]{1,0:T(8,128)(2,1)S(1)} %add_convert_fusion.2), channel_id=1, source_target_pairs={{1,0},{2,1},{3,2},{4,3},{5,4},{6,5},{7,6},{8,7},{9,8},{10,9},{11,1... | collective-permute-start | bytes 786440 | tf_op jit(solution)/shard_map/ppermute | solution.py:29
  101.8 17.1 %copy-start.16 = (f32[1024,128]{1,0:T(8,128)S(1)}, f32[1024,128]{1,0:T(8,128)}, u32[]{:S(2)}) copy-start(f32[1024,128]{1,0:T(8,128)} %convolution_bitcast_fusion) | copy-start | bytes 1572868
  101.8 11.5 %collective-permute-start.7 = (bf16[1024,128]{1,0:T(8,128)(2,1)S(1)}, bf16[1024,128]{1,0:T(8,128)(2,1)S(1)}, u32[]{:S(2)}, u32[]{:S(2)}) collective-permute-start(bf16[1024,128]{1,0:T(8,128)(2,1)S(1)} %add_convert_fusion.5), channel_id=1, source_target_pairs={{1,0},{2,1},{3,2},{4,3},{5,4},{6,5},{7,6},{8,7},{9,8},{10,9},{11,1... | collective-permute-start | bytes 786440 | tf_op jit(solution)/shard_map/ppermute | solution.py:29
  107.7 26.6 %copy-start.3 = (bf16[256,4,1024]{0,2,1:T(8,128)(2,1)S(1)}, bf16[256,4,1024]{0,2,1:T(8,128)(2,1)}, u32[]{:S(2)}) copy-start(bf16[256,4,1024]{0,2,1:T(8,128)(2,1)} %get-tuple-element.30) | copy-start | bytes 6291460
  107.7 11.2 %collective-permute-start.11 = (bf16[1024,128]{1,0:T(8,128)(2,1)S(1)}, bf16[1024,128]{1,0:T(8,128)(2,1)S(1)}, u32[]{:S(2)}, u32[]{:S(2)}) collective-permute-start(bf16[1024,128]{1,0:T(8,128)(2,1)S(1)} %add_convert_fusion.1), channel_id=1, source_target_pairs={{1,0},{2,1},{3,2},{4,3},{5,4},{6,5},{7,6},{8,7},{9,8},{10,9},{11,1... | collective-permute-start | bytes 786440 | tf_op jit(solution)/shard_map/ppermute | solution.py:29
  113.3 11.2 %collective-permute-start.8 = (bf16[1024,128]{1,0:T(8,128)(2,1)S(1)}, bf16[1024,128]{1,0:T(8,128)(2,1)S(1)}, u32[]{:S(2)}, u32[]{:S(2)}) collective-permute-start(bf16[1024,128]{1,0:T(8,128)(2,1)S(1)} %add_convert_fusion.4), channel_id=1, source_target_pairs={{1,0},{2,1},{3,2},{4,3},{5,4},{6,5},{7,6},{8,7},{9,8},{10,9},{11,1... | collective-permute-start | bytes 786440 | tf_op jit(solution)/shard_map/ppermute | solution.py:29
  118.0 17.8 %copy-start.11 = (f32[256,4,128]{0,2,1:T(8,128)S(1)}, f32[256,4,128]{0,2,1:T(8,128)}, u32[]{:S(2)}) copy-start(f32[256,4,128]{0,2,1:T(8,128)} %fusion.46) | copy-start | bytes 1572868
  125.4 18.4 %all-to-all-start = ((bf16[4,256,256]{2,1,0:T(8,128)(2,1)}), bf16[4,256,256]{2,1,0:T(8,128)(2,1)S(1)}, u32[]{:S(2)}, u32[]{:S(2)}) async-start(bf16[4,256,256]{2,1,0:T(8,128)(2,1)} %bitcast.39), calls=%async_computation | async-start | bytes 1048576 | tf_op jit(solution)/shard_map/all_to_all | solution.py:40
  (1 other events, 2.7 us)
where the time goes:
time: 145 us
  matrix products  41.7 us (29%)
  waiting for transfers between devices  35 us (24%)
  starting transfers between devices  28.6 us (20%)
  other arithmetic  21.7 us (15%)
  blocking collectives  11.1 us (8%)
  local copies, waits for them, and re-layouts  5.38 us (4%)
    ppermute x12, waiting for transfers between devices, from_behind(): return lax.ppermute(block, axis, route)  30.1 us
    ppermute x12, starting transfers between devices, from_behind(): return lax.ppermute(block, axis, route)  19.7 us
    dot_general x4, matrix products, per_device(): jnp.einsum('thd,kd->thk', grad_rows, value_rows, preferred_element_type=j...  17.5 us
    convert_element_type x1, other arithmetic, per_device(): (bundle_probs * (grad_prob_list[step] - row_dot[..., None])).astype(jnp.b...  14 us
    all_gather x1, blocking collectives, sent_together(): result = lax.all_gather(both, axis, axis=dim, tiled=True)  11.1 us
    all_to_all x1, starting transfers between devices, summed_on_arrival(): lax.all_to_all(cut_along(array, dim, devices), axis, 0, 0, tiled=True)  8.87 us
    dot_general x4, matrix products, per_device(): jnp.einsum('thk,thd->kd', bundle_probs_low, grad_rows, preferred_element_...  8.56 us
    dot_general x4, matrix products, per_device(): jnp.einsum('thk,kd->thd', grad_scores, bundle_key_rows, preferred_element...  8.07 us
  transfers between devices with their start and end apart: 13, of which 11 were waited for; matrix products, arithmetic and copies ran while one was open for 46% of the time, Pallas kernels for 0%

commit v1 on v0

v1 whole, which is shorter than its diff:
```python
import functools
import math

import jax
import jax.numpy as jnp
from jax import lax
from jax.experimental import pallas as pl
from jax.experimental.pallas import tpu as pltpu
from jax.sharding import PartitionSpec as P

STEPS = 4
F32, BF16 = jnp.float32, jnp.bfloat16
MESH = pl.DeviceIdType.MESH
LOW = -1e30


def dot(a, b, over=(1, 0)):
    dims = (((over[0],), (over[1],)), ((), ()))
    return lax.dot_general(a, b, dims, preferred_element_type=F32)


def kernel(
    inner_size, outer_size, tokens, size, heads,
    place_ref, q_hbm, k_hbm, v_hbm, g_hbm, dq_hbm, dk_hbm, dv_hbm,
    kv, q_rows, g_rows, q_cols, g_cols, probs, grads, maxes, run_max, run_sum, run_dot, dq_cols,
    near, far, core_out, core_in, pair_out, pair_in, ring_out, ring_in, dq_rows,
    load_sem, store_sem,
    ring_s, ring_r, core_s, core_r, pair_s, pair_r,
    back_ring_s, back_ring_r, back_core_s, back_core_r, back_pair_s, back_pair_r,
):
    inner, outer = lax.axis_index("inner"), lax.axis_index("outer")
    other_core = inner + 1 - 2 * (inner % 2)
    other_pair = (inner + 2) % inner_size
    other_both = inner_size - 1 - inner
    after = (outer + 1) % outer_size
    before = (outer + outer_size - 1) % outer_size
    columns = (inner, other_core, other_pair, other_both)
    rows = heads * tokens
    block = tokens // 2
    scale = 1.0 / math.sqrt(size)
    scale2 = scale * math.log2(math.e)

    loads = [
        pltpu.make_async_copy(k_hbm, kv.at[0, 0], load_sem.at[0]),
        pltpu.make_async_copy(v_hbm, kv.at[0, 1], load_sem.at[1]),
    ]
    for h in range(heads):
        there = pl.ds(h * tokens, tokens)
        cut = pl.ds(h * size, size)
        loads.append(pltpu.make_async_copy(q_hbm.at[:, cut], q_rows.at[there], load_sem.at[2 + 2 * h]))
        loads.append(pltpu.make_async_copy(g_hbm.at[:, cut], g_rows.at[there], load_sem.at[3 + 2 * h]))
    for load in loads:
        load.start()

    partners = ((other_core, outer), (other_pair, outer), (inner, after), (inner, before))
    barrier = pltpu.get_barrier_semaphore()
    for partner in partners:
        pl.semaphore_signal(barrier, inc=1, device_id=partner, device_id_type=MESH)
    pl.semaphore_wait(barrier, len(partners))

    def remote(src, dst, send, recv, to):
        return pltpu.make_async_remote_copy(
            src_ref=src, dst_ref=dst, send_sem=send, recv_sem=recv, device_id=to, device_id_type=MESH
        )

    def ring(s):
        return remote(kv.at[4 * s], kv.at[4 * s + 4], ring_s.at[s], ring_r.at[s], (inner, after))

    def core(s, j):
        return remote(
            kv.at[4 * s + 2 * j], kv.at[4 * s + 2 * j + 1], core_s.at[2 * s + j], core_r.at[2 * s + j],
            (other_core, outer),
        )

    def pair(s):
        return remote(kv.at[4 * s], kv.at[4 * s + 2], pair_s.at[s], pair_r.at[s], (other_pair, outer))

    loads[0].wait()
    loads[1].wait()
    ring(0).start()
    pair(0).start()
    core(0, 0).start()

    lane = lax.broadcasted_iota(jnp.int32, (1, rows), 1)
    own_block = 2 * (inner * outer_size + outer)
    q_place = jnp.where((lane // block) % 2 == 0, place_ref[own_block], place_ref[own_block + 1])
    for load in loads[2:]:
        load.wait()
    for h in range(heads):
        there = pl.ds(h * tokens, tokens)
        q_cols[:, there] = q_rows[there, :].T
        g_cols[:, there] = g_rows[there, :].T

    def key_block(s, j):
        return 2 * (columns[j] * outer_size + (outer + outer_size - s) % outer_size)

    def forward(chunks, first=False):
        ids = [4 * s + j for s, j in chunks]
        keys = jnp.concatenate([kv[c, 0] for c in ids], axis=0)
        values = jnp.concatenate([kv[c, 1] for c in ids], axis=0)
        places = [place_ref[key_block(s, j) + b] for s, j in chunks for b in range(2)]
        for h in range(heads):
            at = slice(h * tokens, (h + 1) * tokens)
            place = q_place[:, at]
            bias = [
                jnp.broadcast_to(jnp.where(p <= place, 0.0, LOW).astype(F32), (block, tokens)) for p in places
            ]
            if first:
                row = lax.broadcasted_iota(jnp.int32, (block, tokens), 0)
                col = lax.broadcasted_iota(jnp.int32, (block, tokens), 1) % block
                for b in range(2):
                    ok = places[b] * block + row <= place * block + col
                    bias[b] = jnp.where(ok, 0.0, LOW).astype(F32)
            scores = dot(keys, q_cols[:, at]) * scale2 + jnp.concatenate(bias, axis=0)
            grad_probs = dot(values, g_cols[:, at])
            new_max = jnp.max(scores, axis=0, keepdims=True)
            if not first:
                old_max = run_max[:, at]
                new_max = jnp.maximum(old_max, new_max)
                fade = jnp.exp2(old_max - new_max)
            weights = jnp.exp2(scores - new_max)
            part_sum = jnp.sum(weights, axis=0, keepdims=True)
            part_dot = jnp.sum(weights * grad_probs, axis=0, keepdims=True)
            if not first:
                part_sum += run_sum[:, at] * fade
                part_dot += run_dot[:, at] * fade
            run_sum[:, at] = part_sum
            run_dot[:, at] = part_dot
            run_max[:, at] = new_max
            for n, c in enumerate(ids):
                mine = slice(n * tokens, (n + 1) * tokens)
                probs[c, :, at] = weights[mine].astype(BF16)
                grads[c, :, at] = grad_probs[mine]
                maxes[c, :, at] = new_max

    core(0, 0).wait_recv()
    forward(((0, 0), (0, 1)), first=True)

    def arrive(s, _):
        ring(s - 1).wait_recv()

        @pl.when(s < STEPS - 1)
        def _():
            ring(s).start()

        pair(s).start()
        core(s, 0).start()
        pair(s - 1).wait_recv()
        core(s - 1, 1).start()
        forward(((s, 0), (s - 1, 2)))
        core(s, 0).wait_recv()
        core(s - 1, 1).wait_recv()
        forward(((s, 1), (s - 1, 3)))
        return 0

    lax.fori_loop(1, STEPS, arrive, 0)
    last = STEPS - 1
    pair(last).wait_recv()
    core(last, 1).start()
    core(last, 1).wait_recv()
    forward(((last, 2), (last, 3)))

    inverse = 1.0 / run_sum[...]
    run_sum[...] = inverse
    run_dot[...] = run_dot[...] * inverse
    dq_cols[...] = jnp.zeros_like(dq_cols)

    def backward(ids):
        keys = jnp.concatenate([kv[c, 0] for c in ids], axis=0)
        dk = jnp.zeros((len(ids) * tokens, size), F32)
        dv = jnp.zeros((len(ids) * tokens, size), F32)
        factors = [jnp.exp2(maxes[c] - run_max[...]) * run_sum[...] for c in ids]
        for h in range(heads):
            at = slice(h * tokens, (h + 1) * tokens)
            low, slopes = [], []
            for c, factor in zip(ids, factors):
                weights = probs[c, :, at].astype(F32) * factor[:, at]
                low.append(weights.astype(BF16))
                slopes.append((weights * (grads[c, :, at] - run_dot[:, at])).astype(BF16))
            low = jnp.concatenate(low, axis=0)
            slopes = jnp.concatenate(slopes, axis=0)
            dv += dot(low, g_rows[at, :])
            dk += dot(slopes, q_rows[at, :])
            dq_cols[:, at] += dot(keys, slopes, (0, 0))
        dk = dk * scale
        return [
            (dk[n * tokens : (n + 1) * tokens], dv[n * tokens : (n + 1) * tokens]) for n in range(len(ids))
        ]

    def back_core(s, j):
        n = 2 * s + j
        return remote(core_out.at[n], core_in.at[n], back_core_s.at[n], back_core_r.at[n], (other_core, outer))

    def back_pair(s):
        return remote(pair_out.at[s], pair_in.at[s], back_pair_s.at[s], back_pair_r.at[s], (other_pair, outer))

    def back_ring(s):
        return remote(ring_out.at[s], ring_in.at[s - 1], back_ring_s.at[s], back_ring_r.at[s - 1], (inner, before))

    def total(s):
        back_core(s, 0).wait_recv()
        back_pair(s).wait_recv()
        return near[s] + core_in[2 * s].astype(F32) + pair_in[s].astype(F32)

    def arrived(s):
        return pltpu.make_async_remote_copy(
            src_ref=ring_out.at[s], dst_ref=ring_in.at[s], send_sem=back_ring_s.at[s], recv_sem=back_ring_r.at[s],
            device_id=(inner, before), device_id_type=MESH,
        )

    def settle(s):
        whole = total(s)
        if s < STEPS - 1:
            arrived(s).wait_recv()
            whole = whole + ring_in[s].astype(F32)
        ring_out[s] = whole.astype(BF16)
        if s > 0:
            back_ring(s).start()

    def leave(n, _):
        s = STEPS - 1 - n
        pairs = backward((4 * s + 3, 4 * s + 2))
        core_out[2 * s + 1, 0] = pairs[0][0].astype(BF16)
        core_out[2 * s + 1, 1] = pairs[0][1].astype(BF16)
        back_core(s, 1).start()
        far[0] = pairs[1][0]
        far[1] = pairs[1][1]
        pairs = backward((4 * s + 1, 4 * s))
        core_out[2 * s, 0] = pairs[0][0].astype(BF16)
        core_out[2 * s, 1] = pairs[0][1].astype(BF16)
        back_core(s, 0).start()
        near[s, 0] = pairs[1][0]
        near[s, 1] = pairs[1][1]
        back_core(s, 1).wait_recv()
        pair_out[s] = (far[...] + core_in[2 * s + 1].astype(F32)).astype(BF16)
        back_pair(s).start()

        @pl.when(n == 2)
        def _():
            settle(STEPS - 1)

        return 0

    lax.fori_loop(0, STEPS, leave, 0)

    for h in range(heads):
        part = dq_cols[:, h * tokens : (h + 1) * tokens] * scale
        dq_rows[:, h * size : (h + 1) * size] = part.T.astype(BF16)
    store_dq = pltpu.make_async_copy(dq_rows, dq_hbm, store_sem.at[0])
    store_dq.start()
    for s in reversed(range(STEPS - 1)):
        settle(s)
    store_dk = pltpu.make_async_copy(ring_out.at[0, 0], dk_hbm, store_sem.at[1])
    store_dv = pltpu.make_async_copy(ring_out.at[0, 1], dv_hbm, store_sem.at[2])
    store_dk.start()
    store_dv.start()
    for s in range(STEPS):
        pair(s).wait_send()
        back_pair(s).wait_send()
        for j in range(2):
            core(s, j).wait_send()
            back_core(s, j).wait_send()
        if s < STEPS - 1:
            ring(s).wait_send()
            back_ring(s + 1).wait_send()
    store_dq.wait()
    store_dk.wait()
    store_dv.wait()


def per_device(queries, keys, values, out_grad, block_place):
    tokens, size = keys.shape
    heads = queries.shape[1] // size
    rows = heads * tokens
    chunks = 4 * STEPS
    dma = pltpu.SemaphoreType.DMA
    hbm = pl.BlockSpec(memory_space=pl.ANY)
    kept = lambda *shape: pltpu.VMEM(shape, F32)
    low = lambda *shape: pltpu.VMEM(shape, BF16)
    body = functools.partial(
        kernel, lax.axis_size("inner"), lax.axis_size("outer"), tokens, size, heads
    )
    return pl.pallas_call(
        body,
        out_shape=(
            jax.ShapeDtypeStruct(queries.shape, BF16),
            jax.ShapeDtypeStruct(keys.shape, BF16),
            jax.ShapeDtypeStruct(values.shape, BF16),
        ),
        in_specs=[pl.BlockSpec(memory_space=pltpu.SMEM), hbm, hbm, hbm, hbm],
        out_specs=(hbm, hbm, hbm),
        scratch_shapes=[
            low(chunks, 2, tokens, size),
            low(rows, size), low(rows, size), low(size, rows), low(size, rows),
            low(chunks, tokens, rows), kept(chunks, tokens, rows), kept(chunks, 1, rows),
            kept(1, rows), kept(1, rows), kept(1, rows), kept(size, rows),
            kept(STEPS, 2, tokens, size), kept(2, tokens, size),
            low(2 * STEPS, 2, tokens, size), low(2 * STEPS, 2, tokens, size),
            low(STEPS, 2, tokens, size), low(STEPS, 2, tokens, size),
            low(STEPS, 2, tokens, size), low(STEPS, 2, tokens, size),
            low(tokens, heads * size),
            dma((2 + 2 * heads,)), dma((3,)),
            dma((STEPS,)), dma((STEPS,)), dma((2 * STEPS,)), dma((2 * STEPS,)), dma((STEPS,)), dma((STEPS,)),
            dma((STEPS,)), dma((STEPS,)), dma((2 * STEPS,)), dma((2 * STEPS,)), dma((STEPS,)), dma((STEPS,)),
        ],
        compiler_params=pltpu.CompilerParams(
            collective_id=0, has_side_effects=True, vmem_limit_bytes=58 * 2**20
        ),
        cost_estimate=pl.CostEstimate(
            flops=10 * rows * chunks * tokens * size, bytes_accessed=6 * tokens * size * (heads + 1), transcendentals=rows * chunks * tokens
        ),
        name="attention_backward",
    )(block_place, queries, keys, values, out_grad)


def solution(mesh):
    placed = P(("inner", "outer"), None)
    return jax.shard_map(
        per_device,
        mesh=mesh,
        in_specs=(placed, placed, placed, placed, P()),
        out_specs=(placed, placed, placed),
        check_vma=False,
    )
```

time: 145 us -> 60.9 us (0.42)
  Pallas kernels: 0 us -> 56.9 us
  matrix products: 41.7 us -> 0 us
  waiting for transfers between devices: 35 us -> 0 us
  starting transfers between devices: 28.6 us -> 0 us
  other arithmetic: 21.7 us -> 0 us
  blocking collectives: 11.1 us -> 0 us
  local copies, waits for them, and re-layouts: 5.38 us -> 3.2 us
    pallas_call x0 -> x1, Pallas kernels: none -> 56.9 us  [per_device(): pl.pallas_call(body, out_shape=(jax.ShapeDtypeStruct(queries.shape, BF16)...]
    dot_general x20 -> x0, matrix products: 41.7 us -> none  [the longest x4 17.5 us: per_device(): jnp.einsum('thd,kd->thk', grad_rows, value_rows, preferred_element_type=j...]
    ppermute x12 -> x0, waiting for transfers between devices: 30.1 us -> none  [from_behind(): return lax.ppermute(block, axis, route)]
    ppermute x12 -> x0, starting transfers between devices: 19.7 us -> none  [from_behind(): return lax.ppermute(block, axis, route)]
    convert_element_type x5 -> x0, other arithmetic: 14.2 us -> none  [the longest x1 14 us: per_device(): (bundle_probs * (grad_prob_list[step] - row_dot[..., None])).astype(jnp.b...]
    all_gather x1 -> x0, blocking collectives: 11.1 us -> none  [sent_together(): result = lax.all_gather(both, axis, axis=dim, tiled=True)]
    all_to_all x1 -> x0, starting transfers between devices: 8.87 us -> none  [summed_on_arrival(): lax.all_to_all(cut_along(array, dim, devices), axis, 0, 0, tiled=True)]
    all_to_all x1 -> x0, waiting for transfers between devices: 4.89 us -> none  [summed_on_arrival(): lax.all_to_all(cut_along(array, dim, devices), axis, 0, 0, tiled=True)]
  transfers between devices with their start and end apart: 13 -> 0, of which waited for: 11 -> 0; matrix products, arithmetic and copies ran while one was open for 46% -> 0% of each run, Pallas kernels for 0% -> 0%
where the time goes in v1:
time: 60.9 us; the launch traced here: 60.7 us
  Pallas kernels  56.9 us (93%)
  local copies, waits for them, and re-layouts  3.2 us (5%)
  between operations  0.65 us (1%)
    pallas_call x1, Pallas kernels, per_device(): pl.pallas_call(body, out_shape=(jax.ShapeDtypeStruct(queries.shape, BF16)...  56.9 us
    unnamed x7, local copies, waits for them, and re-layouts  3.2 us

profile of v1, /device:TPU:1, one launch (start us, length us, event | category | flops | bytes accessed | tf_op | source)
XLA Modules:
  0.0 60.7 jit_solution(2824243360136633912)
XLA Ops:
  0.6 56.9 %attention_backward.1 = (bf16[256,512]{1,0:T(8,128)(2,1)}, bf16[256,128]{1,0:T(8,128)(2,1)}, bf16[256,128]{1,0:T(8,128)(2,1)}) custom-call(s32[512]{0:T(512)} %place_ref.1, bf16[256,512]{1,0:T(8,128)(2,1)} %q_hbm.1, bf16[256,128]{1,0:T(8,128)(2,1)} %k_hbm.1, bf16[256,128]{1,0:T(8,128)(2,1)} %v_hbm.1, bf16[256,512]{1,0:T(8,128)(2,1)} %g_hbm.1), custom_call_target="tpu_custom_call" | custom-call | flops 5368709120 | bytes 983040 | tf_op jit(solution)/shard_map/attention_backward/pallas_call | solution.py:283
  57.5 0.0 copy-start.1
  57.5 1.7 %copy.11 = bf16[256,512]{1,0:T(8,128)(2,1)} copy(bf16[256,512]{1,0:T(8,128)(2,1)} %get-tuple-element.6) | data formatting | bytes 524288
  59.2 0.0 copy-done.1
  59.2 0.0 copy-start
  59.2 0.6 %copy.12 = bf16[256,128]{1,0:T(8,128)(2,1)} copy(bf16[256,128]{1,0:T(8,128)(2,1)S(1)} %copy-done.1) | data formatting | bytes 131072
  59.8 0.2 copy-done
  60.1 0.6 %copy.13 = bf16[256,128]{1,0:T(8,128)(2,1)} copy(bf16[256,128]{1,0:T(8,128)(2,1)S(1)} %copy-done) | data formatting | bytes 131072
Async XLA Ops:
  57.5 1.7 %copy-start.1 = (bf16[256,128]{1,0:T(8,128)(2,1)S(1)}, bf16[256,128]{1,0:T(8,128)(2,1)}, u32[]{:S(2)}) copy-start(bf16[256,128]{1,0:T(8,128)(2,1)} %get-tuple-element.7) | copy-start | bytes 196612
  59.2 0.9 %copy-start = (bf16[256,128]{1,0:T(8,128)(2,1)S(1)}, bf16[256,128]{1,0:T(8,128)(2,1)}, u32[]{:S(2)}) copy-start(bf16[256,128]{1,0:T(8,128)(2,1)} %get-tuple-element.8) | copy-start | bytes 196612

commit v2 on v1

v2 whole, which is shorter than its diff:
```python
import functools
import math

import jax
import jax.numpy as jnp
from jax import lax
from jax.experimental import pallas as pl
from jax.experimental.pallas import tpu as pltpu
from jax.sharding import PartitionSpec as P

STEPS = 4
LINE = 8
DIAG = False
SWAP = True
F32, BF16 = jnp.float32, jnp.bfloat16
MESH = pl.DeviceIdType.MESH
LOW = -1e30


def dot(a, b, over=(1, 0)):
    dims = (((over[0],), (over[1],)), ((), ()))
    return lax.dot_general(a, b, dims, preferred_element_type=F32)


def kernel(
    inner_size, outer_size, tokens, size, heads,
    place_ref, q_hbm, k_hbm, v_hbm, g_hbm, dq_hbm, dk_hbm, dv_hbm,
    kv, q_nat, g_nat, q_cols, g_cols, probs, grads, maxes, stats, stats_in, dq_cols, dq_in,
    near, pair_out, pair_in, ring_out, ring_in, diag_in, dq_rows,
    load_sem, store_sem, q_s, q_r, stats_s, stats_r, dq_s, dq_r,
    ring_s, ring_r, pair_s, pair_r, diag_s, diag_r,
    back_ring_s, back_ring_r, back_pair_s, back_pair_r, back_diag_s, back_diag_r,
):
    inner, outer = lax.axis_index("inner"), lax.axis_index("outer")
    core, depth = inner % 2, outer % LINE
    other_core = inner + 1 - 2 * core
    other_pair = (inner + 2) % inner_size
    crossing = core if SWAP else 0 * core
    after_side = (inner + 2 * crossing * (depth // (LINE - 1))) % inner_size
    before_side = (inner + 2 * crossing * ((LINE - 1 - depth) // (LINE - 1))) % inner_size
    after = (after_side, (outer + 1) % outer_size)
    before = (before_side, (outer + outer_size - 1) % outer_size)
    after_pair = ((after_side + 2) % inner_size, after[1])
    before_pair = ((before_side + 2) % inner_size, before[1])
    mate = (other_core, outer)
    pair = (other_pair, outer)
    own_rows = heads * tokens
    rows = 2 * own_rows
    block = tokens // 2
    scale = 1.0 / math.sqrt(size)
    scale2 = scale * math.log2(math.e)

    loads = [
        pltpu.make_async_copy(src, dst, load_sem.at[n])
        for n, (src, dst) in enumerate(
            ((k_hbm, kv.at[0, 0]), (v_hbm, kv.at[0, 1]), (q_hbm, q_nat.at[0]), (g_hbm, g_nat.at[0]))
        )
    ]
    for load in loads:
        load.start()

    partners = [mate, pair, after, before] + ([after_pair, before_pair] if DIAG else [])
    barrier = pltpu.get_barrier_semaphore()
    for partner in partners:
        pl.semaphore_signal(barrier, inc=1, device_id=partner, device_id_type=MESH)
    pl.semaphore_wait(barrier, len(partners))

    def remote(src, dst, send, recv, to):
        return pltpu.make_async_remote_copy(
            src_ref=src, dst_ref=dst, send_sem=send, recv_sem=recv, device_id=to, device_id_type=MESH
        )

    def ring(s, p):
        return remote(kv.at[2 * s, p], kv.at[2 * s + 2, p], ring_s.at[2 * s + p], ring_r.at[2 * s + p], after)

    def side(s, p):
        return remote(kv.at[2 * s, p], kv.at[2 * s + 1, p], pair_s.at[2 * s + p], pair_r.at[2 * s + p], pair)

    def diag(p):
        last = 2 * STEPS
        return remote(kv.at[last - 4, p], kv.at[last - 1, p], diag_s.at[p], diag_r.at[p], after_pair)

    q_over = remote(q_hbm, q_nat.at[1], q_s.at[0], q_r.at[0], mate)
    g_over = remote(g_hbm, g_nat.at[1], q_s.at[1], q_r.at[1], mate)
    for p in range(2):
        loads[p].wait()
        ring(0, p).start()
        side(0, p).start()
    q_over.start()
    g_over.start()

    lane = lax.broadcasted_iota(jnp.int32, (1, own_rows), 1)

    def row_places(side_inner):
        first_block = 2 * (side_inner * outer_size + outer)
        return jnp.where((lane // block) % 2 == 0, place_ref[first_block], place_ref[first_block + 1])

    q_place = jnp.concatenate([row_places(inner), row_places(other_core)], axis=1)

    def turn(n):
        for h in range(heads):
            there = pl.ds(n * own_rows + h * tokens, tokens)
            q_cols[:, there] = q_nat[n, :, h * size : (h + 1) * size].T
            g_cols[:, there] = g_nat[n, :, h * size : (h + 1) * size].T

    loads[2].wait()
    loads[3].wait()
    turn(0)
    q_over.wait_recv()
    g_over.wait_recv()
    turn(1)

    def key_block(s, j):
        crossed = jnp.where(depth < s, crossing, 0)
        column = (inner + 2 * crossed + 2 * j) % inner_size
        return 2 * (column * outer_size + (outer + outer_size - s) % outer_size)

    def forward(s, j, first=False):
        c = 2 * s + j
        keys, values = kv[c, 0], kv[c, 1]
        places = [place_ref[key_block(s, j) + b] for b in range(2)]
        for t in range(rows // tokens):
            at = slice(t * tokens, (t + 1) * tokens)
            place = q_place[:, at]
            bias = [jnp.broadcast_to(jnp.where(p <= place, 0.0, LOW).astype(F32), (block, tokens)) for p in places]
            if first and t < heads:
                row = lax.broadcasted_iota(jnp.int32, (block, tokens), 0)
                col = lax.broadcasted_iota(jnp.int32, (block, tokens), 1) % block
                for b in range(2):
                    ok = places[b] * block + row <= place * block + col
                    bias[b] = jnp.where(ok, 0.0, LOW).astype(F32)
            scores = dot(keys, q_cols[:, at]) * scale2 + jnp.concatenate(bias, axis=0)
            grad_probs = dot(values, g_cols[:, at])
            new_max = jnp.max(scores, axis=0, keepdims=True)
            if not first:
                old_max = stats[0:1, at]
                new_max = jnp.maximum(old_max, new_max)
                fade = jnp.exp2(old_max - new_max)
            weights = jnp.exp2(scores - new_max)
            part_sum = jnp.sum(weights, axis=0, keepdims=True)
            part_dot = jnp.sum(weights * grad_probs, axis=0, keepdims=True)
            if not first:
                part_sum += stats[1:2, at] * fade
                part_dot += stats[2:3, at] * fade
            stats[0:1, at] = new_max
            stats[1:2, at] = part_sum
            stats[2:3, at] = part_dot
            probs[c, :, at] = weights.astype(BF16)
            grads[c, :, at] = grad_probs
            maxes[c, :, at] = new_max

    forward(0, 0, first=True)

    def arrive(s, _):
        for p in range(2):
            ring(s - 1, p).wait_recv()

            @pl.when(s < STEPS - 1)
            def _():
                ring(s, p).start()
                side(s, p).start()
                if DIAG:
                    @pl.when(s == STEPS - 2)
                    def _():
                        diag(p).start()
            if not DIAG:
                @pl.when(s == STEPS - 1)
                def _():
                    side(s, p).start()

        forward(s, 0)
        side(s - 1, 0).wait_recv()
        side(s - 1, 1).wait_recv()
        forward(s - 1, 1)
        return 0

    lax.fori_loop(1, STEPS, arrive, 0)
    last = STEPS - 1
    for p in range(2):
        (diag(p) if DIAG else side(last, p)).wait_recv()
    forward(last, 1)

    def swap_stats(n):
        here = pl.ds(n * own_rows, own_rows)
        there = pl.ds((1 - n) * own_rows, own_rows)
        return remote(stats.at[:, here], stats_in.at[:, there], stats_s.at[n], stats_r.at[n], mate)

    for n in range(2):
        swap_stats(n).start()
    dq_cols[...] = jnp.zeros_like(dq_cols)
    for n in range(2):
        swap_stats(n).wait()
    top = jnp.maximum(stats[0:1, :], stats_in[0:1, :])
    here, there = jnp.exp2(stats[0:1, :] - top), jnp.exp2(stats_in[0:1, :] - top)
    inverse = 1.0 / (stats[1:2, :] * here + stats_in[1:2, :] * there)
    mean = (stats[2:3, :] * here + stats_in[2:3, :] * there) * inverse
    stats[0:1, :] = top
    stats[1:2, :] = inverse
    stats[2:3, :] = mean

    def backward(c):
        keys = kv[c, 0]
        dk = jnp.zeros((tokens, size), F32)
        dv = jnp.zeros((tokens, size), F32)
        factor = jnp.exp2(maxes[c] - stats[0:1, :]) * stats[1:2, :]
        for t in range(rows // tokens):
            at = slice(t * tokens, (t + 1) * tokens)
            n, h = t // heads, t % heads
            cut = slice(h * size, (h + 1) * size)
            weights = probs[c, :, at].astype(F32) * factor[:, at]
            slopes = (weights * (grads[c, :, at] - stats[2:3, at])).astype(BF16)
            dv += dot(weights.astype(BF16), g_nat[n, :, cut])
            dk += dot(slopes, q_nat[n, :, cut])
            dq_cols[:, at] += dot(keys, slopes, (0, 0))
        return dk * scale, dv

    def back_side(s):
        return remote(pair_out.at[s], pair_in.at[s], back_pair_s.at[s], back_pair_r.at[s], pair)

    def back_diag():
        return remote(pair_out.at[last], diag_in, back_diag_s.at[0], back_diag_r.at[0], before_pair)

    def back_ring(s, p):
        n = 2 * s + p
        return remote(ring_out.at[s, p], ring_in.at[s - 1, p], back_ring_s.at[n], back_ring_r.at[n - 2], before)

    def arrived(s, p):
        n = 2 * s + p
        return remote(ring_out.at[s, p], ring_in.at[s, p], back_ring_s.at[n], back_ring_r.at[n], before)

    def settle(s):
        direct = DIAG and s == last
        if not direct:
            back_side(s).wait_recv()
        if DIAG and s == last - 1:
            back_diag().wait_recv()
        for p in range(2):
            whole = near[s, p]
            if not direct:
                whole = whole + pair_in[s, p].astype(F32)
            if DIAG and s == last - 1:
                whole = whole + diag_in[p].astype(F32)
            if s < last:
                arrived(s, p).wait_recv()
                whole = whole + ring_in[s, p].astype(F32)
            ring_out[s, p] = whole.astype(BF16)
            if s > 0:
                back_ring(s, p).start()

    def leave(n, _):
        s = last - n
        dk, dv = backward(2 * s + 1)
        pair_out[s, 0] = dk.astype(BF16)
        pair_out[s, 1] = dv.astype(BF16)
        if DIAG:
            @pl.when(n == 0)
            def _():
                back_diag().start()

            @pl.when(n > 0)
            def _():
                back_side(s).start()
        else:
            back_side(s).start()
        dk, dv = backward(2 * s)
        near[s, 0] = dk
        near[s, 1] = dv

        @pl.when(n == (0 if DIAG else 2))
        def _():
            settle(last)

        return 0

    lax.fori_loop(0, STEPS, leave, 0)

    dq_over = remote(dq_cols.at[:, pl.ds(own_rows, own_rows)], dq_in, dq_s.at[0], dq_r.at[0], mate)
    dq_over.start()
    settle(last - 1)
    dq_over.wait_recv()
    for h in range(heads):
        there = slice(h * tokens, (h + 1) * tokens)
        part = (dq_cols[:, there] + dq_in[:, there]) * scale
        dq_rows[:, h * size : (h + 1) * size] = part.T.astype(BF16)
    store_dq = pltpu.make_async_copy(dq_rows, dq_hbm, store_sem.at[0])
    store_dq.start()
    for s in reversed(range(last - 1)):
        settle(s)
    store_dk = pltpu.make_async_copy(ring_out.at[0, 0], dk_hbm, store_sem.at[1])
    store_dv = pltpu.make_async_copy(ring_out.at[0, 1], dv_hbm, store_sem.at[2])
    store_dk.start()
    store_dv.start()
    q_over.wait_send()
    g_over.wait_send()
    dq_over.wait_send()
    for s in range(STEPS):
        for p in range(2):
            if s < last:
                ring(s, p).wait_send()
                back_ring(s + 1, p).wait_send()
            if s < last or not DIAG:
                side(s, p).wait_send()
            if s == last and DIAG:
                diag(p).wait_send()
        if s < last or not DIAG:
            back_side(s).wait_send()
        else:
            back_diag().wait_send()
    store_dq.wait()
    store_dk.wait()
    store_dv.wait()


def per_device(queries, keys, values, out_grad, block_place):
    tokens, size = keys.shape
    heads = queries.shape[1] // size
    own_rows = heads * tokens
    rows = 2 * own_rows
    chunks = 2 * STEPS
    dma = lambda count: pltpu.SemaphoreType.DMA((count,))
    hbm = pl.BlockSpec(memory_space=pl.ANY)
    kept = lambda *shape: pltpu.VMEM(shape, F32)
    low = lambda *shape: pltpu.VMEM(shape, BF16)
    body = functools.partial(
        kernel, lax.axis_size("inner"), lax.axis_size("outer"), tokens, size, heads
    )
    return pl.pallas_call(
        body,
        out_shape=(
            jax.ShapeDtypeStruct(queries.shape, BF16),
            jax.ShapeDtypeStruct(keys.shape, BF16),
            jax.ShapeDtypeStruct(values.shape, BF16),
        ),
        in_specs=[pl.BlockSpec(memory_space=pltpu.SMEM), hbm, hbm, hbm, hbm],
        out_specs=(hbm, hbm, hbm),
        scratch_shapes=[
            low(chunks, 2, tokens, size),
            low(2, tokens, heads * size), low(2, tokens, heads * size), low(size, rows), low(size, rows),
            low(chunks, tokens, rows), kept(chunks, tokens, rows), kept(chunks, 1, rows),
            kept(8, rows), kept(8, rows), kept(size, rows), kept(size, own_rows),
            kept(STEPS, 2, tokens, size),
            low(STEPS, 2, tokens, size), low(STEPS, 2, tokens, size),
            low(STEPS, 2, tokens, size), low(STEPS, 2, tokens, size), low(2, tokens, size),
            low(tokens, heads * size),
            dma(4), dma(3), dma(2), dma(2), dma(2), dma(2), dma(1), dma(1),
            dma(chunks), dma(chunks), dma(chunks), dma(chunks), dma(2), dma(2),
            dma(chunks), dma(chunks), dma(STEPS), dma(STEPS), dma(1), dma(1),
        ],
        compiler_params=pltpu.CompilerParams(
            collective_id=0, has_side_effects=True, vmem_limit_bytes=58 * 2**20
        ),
        cost_estimate=pl.CostEstimate(
            flops=10 * rows * chunks * tokens * size,
            bytes_accessed=6 * tokens * size * (heads + 1),
            transcendentals=rows * chunks * tokens,
        ),
        name="attention_backward",
    )(block_place, queries, keys, values, out_grad)


def solution(mesh):
    placed = P(("inner", "outer"), None)
    return jax.shard_map(
        per_device,
        mesh=mesh,
        in_specs=(placed, placed, placed, placed, P()),
        out_specs=(placed, placed, placed),
        check_vma=False,
    )
```

time: 60.9 us -> 52.6 us (0.86)
  Pallas kernels: 56.9 us -> 48.6 us
    pallas_call x1, Pallas kernels: 56.9 us -> 48.6 us  [per_device(): pl.pallas_call(body, out_shape=(jax.ShapeDtypeStruct(queries.shape, BF16)...]
where the time goes in v2:
time: 52.6 us; the launch traced here: 52.5 us
  Pallas kernels  48.6 us (92%)
  local copies, waits for them, and re-layouts  3.2 us (6%)
  between operations  0.65 us (1%)
    pallas_call x1, Pallas kernels, per_device(): pl.pallas_call(body, out_shape=(jax.ShapeDtypeStruct(queries.shape, BF16)...  48.6 us
    unnamed x7, local copies, waits for them, and re-layouts  3.2 us

profile of v2, /device:TPU:1, one launch (start us, length us, event | category | flops | bytes accessed | tf_op | source)
XLA Modules:
  0.0 52.5 jit_solution(18154529946296395390)
XLA Ops:
  0.6 48.6 %attention_backward.1 = (bf16[256,512]{1,0:T(8,128)(2,1)}, bf16[256,128]{1,0:T(8,128)(2,1)}, bf16[256,128]{1,0:T(8,128)(2,1)}) custom-call(s32[512]{0:T(512)} %place_ref.1, bf16[256,512]{1,0:T(8,128)(2,1)} %q_hbm.1, bf16[256,128]{1,0:T(8,128)(2,1)} %k_hbm.1, bf16[256,128]{1,0:T(8,128)(2,1)} %v_hbm.1, bf16[256,512]{1,0:T(8,128)(2,1)} %g_hbm.1), custom_call_target="tpu_custom_call" | custom-call | flops 5368709120 | bytes 983040 | tf_op jit(solution)/shard_map/attention_backward/pallas_call | solution.py:327
  49.2 0.0 copy-start.1
  49.3 1.7 %copy.11 = bf16[256,512]{1,0:T(8,128)(2,1)} copy(bf16[256,512]{1,0:T(8,128)(2,1)} %get-tuple-element.6) | data formatting | bytes 524288
  51.0 0.0 copy-done.1
  51.0 0.0 copy-start
  51.0 0.6 %copy.12 = bf16[256,128]{1,0:T(8,128)(2,1)} copy(bf16[256,128]{1,0:T(8,128)(2,1)S(1)} %copy-done.1) | data formatting | bytes 131072
  51.6 0.2 copy-done
  51.8 0.6 %copy.13 = bf16[256,128]{1,0:T(8,128)(2,1)} copy(bf16[256,128]{1,0:T(8,128)(2,1)S(1)} %copy-done) | data formatting | bytes 131072
Async XLA Ops:
  49.2 1.7 %copy-start.1 = (bf16[256,128]{1,0:T(8,128)(2,1)S(1)}, bf16[256,128]{1,0:T(8,128)(2,1)}, u32[]{:S(2)}) copy-start(bf16[256,128]{1,0:T(8,128)(2,1)} %get-tuple-element.7) | copy-start | bytes 196612
  51.0 0.9 %copy-start = (bf16[256,128]{1,0:T(8,128)(2,1)S(1)}, bf16[256,128]{1,0:T(8,128)(2,1)}, u32[]{:S(2)}) copy-start(bf16[256,128]{1,0:T(8,128)(2,1)} %get-tuple-element.8) | copy-start | bytes 196612

commit v3 on v2

--- a/solution.py
+++ b/solution.py
@@ -10,8 +10,7 @@
 
 STEPS = 4
 LINE = 8
-DIAG = False
-SWAP = True
+PIECES = 4
 F32, BF16 = jnp.float32, jnp.bfloat16
 MESH = pl.DeviceIdType.MESH
 LOW = -1e30
@@ -24,24 +23,20 @@
 
 def kernel(
     inner_size, outer_size, tokens, size, heads,
-    place_ref, q_hbm, k_hbm, v_hbm, g_hbm, dq_hbm, dk_hbm, dv_hbm,
+    place_ref, q_hbm, k_hbm, v_hbm, g_hbm, dq_ref, dk_ref, dv_ref,
     kv, q_nat, g_nat, q_cols, g_cols, probs, grads, maxes, stats, stats_in, dq_cols, dq_in,
-    near, pair_out, pair_in, ring_out, ring_in, diag_in, dq_rows,
-    load_sem, store_sem, q_s, q_r, stats_s, stats_r, dq_s, dq_r,
-    ring_s, ring_r, pair_s, pair_r, diag_s, diag_r,
-    back_ring_s, back_ring_r, back_pair_s, back_pair_r, back_diag_s, back_diag_r,
+    near, pair_out, pair_in, ring_out, ring_in,
+    load_sem, q_s, q_r, stats_s, stats_r, dq_s, dq_r,
+    ring_s, ring_r, pair_s, pair_r, back_ring_s, back_ring_r, back_pair_s, back_pair_r,
 ):
     inner, outer = lax.axis_index("inner"), lax.axis_index("outer")
     core, depth = inner % 2, outer % LINE
     other_core = inner + 1 - 2 * core
     other_pair = (inner + 2) % inner_size
-    crossing = core if SWAP else 0 * core
-    after_side = (inner + 2 * crossing * (depth // (LINE - 1))) % inner_size
-    before_side = (inner + 2 * crossing * ((LINE - 1 - depth) // (LINE - 1))) % inner_size
+    after_side = (inner + 2 * core * (depth // (LINE - 1))) % inner_size
+    before_side = (inner + 2 * core * ((LINE - 1 - depth) // (LINE - 1))) % inner_size
     after = (after_side, (outer + 1) % outer_size)
     before = (before_side, (outer + outer_size - 1) % outer_size)
-    after_pair = ((after_side + 2) % inner_size, after[1])
-    before_pair = ((before_side + 2) % inner_size, before[1])
     mate = (other_core, outer)
     pair = (other_pair, outer)
     own_rows = heads * tokens
@@ -59,7 +54,7 @@
     for load in loads:
         load.start()
 
-    partners = [mate, pair, after, before] + ([after_pair, before_pair] if DIAG else [])
+    partners = [mate, pair, after, before]
     barrier = pltpu.get_barrier_semaphore()
     for partner in partners:
         pl.semaphore_signal(barrier, inc=1, device_id=partner, device_id_type=MESH)
@@ -70,21 +65,26 @@
             src_ref=src, dst_ref=dst, send_sem=send, recv_sem=recv, device_id=to, device_id_type=MESH
         )
 
+    def piece(ref, p):
+        per = PIECES // 2
+        length = tokens // per
+        return ref.at[p // per, pl.ds((p % per) * length, length)]
+
     def ring(s, p):
-        return remote(kv.at[2 * s, p], kv.at[2 * s + 2, p], ring_s.at[2 * s + p], ring_r.at[2 * s + p], after)
+        n = PIECES * s + p
+        return remote(piece(kv.at[2 * s], p), piece(kv.at[2 * s + 2], p), ring_s.at[n], ring_r.at[n], after)
 
     def side(s, p):
-        return remote(kv.at[2 * s, p], kv.at[2 * s + 1, p], pair_s.at[2 * s + p], pair_r.at[2 * s + p], pair)
-
-    def diag(p):
-        last = 2 * STEPS
-        return remote(kv.at[last - 4, p], kv.at[last - 1, p], diag_s.at[p], diag_r.at[p], after_pair)
+        n = PIECES * s + p
+        return remote(piece(kv.at[2 * s], p), piece(kv.at[2 * s + 1], p), pair_s.at[n], pair_r.at[n], pair)
 
     q_over = remote(q_hbm, q_nat.at[1], q_s.at[0], q_r.at[0], mate)
     g_over = remote(g_hbm, g_nat.at[1], q_s.at[1], q_r.at[1], mate)
-    for p in range(2):
-        loads[p].wait()
+    loads[0].wait()
+    loads[1].wait()
+    for p in range(PIECES):
         ring(0, p).start()
+    for p in range(PIECES):
         side(0, p).start()
     q_over.start()
     g_over.start()
@@ -111,7 +111,7 @@
     turn(1)
 
     def key_block(s, j):
-        crossed = jnp.where(depth < s, crossing, 0)
+        crossed = jnp.where(depth < s, core, 0)
         column = (inner + 2 * crossed + 2 * j) % inner_size
         return 2 * (column * outer_size + (outer + outer_size - s) % outer_size)
 
@@ -152,32 +152,25 @@
     forward(0, 0, first=True)
 
     def arrive(s, _):
-        for p in range(2):
+        for p in range(PIECES):
             ring(s - 1, p).wait_recv()
 
             @pl.when(s < STEPS - 1)
             def _():
                 ring(s, p).start()
-                side(s, p).start()
-                if DIAG:
-                    @pl.when(s == STEPS - 2)
-                    def _():
-                        diag(p).start()
-            if not DIAG:
-                @pl.when(s == STEPS - 1)
-                def _():
-                    side(s, p).start()
+
+            side(s, p).start()
 
         forward(s, 0)
-        side(s - 1, 0).wait_recv()
-        side(s - 1, 1).wait_recv()
+        for p in range(PIECES):
+            side(s - 1, p).wait_recv()
         forward(s - 1, 1)
         return 0
 
     lax.fori_loop(1, STEPS, arrive, 0)
     last = STEPS - 1
-    for p in range(2):
-        (diag(p) if DIAG else side(last, p)).wait_recv()
+    for p in range(PIECES):
+        side(last, p).wait_recv()
     forward(last, 1)
 
     def swap_stats(n):
@@ -217,62 +210,54 @@
     def back_side(s):
         return remote(pair_out.at[s], pair_in.at[s], back_pair_s.at[s], back_pair_r.at[s], pair)
 
-    def back_diag():
-        return remote(pair_out.at[last], diag_in, back_diag_s.at[0], back_diag_r.at[0], before_pair)
-
     def back_ring(s, p):
-        n = 2 * s + p
-        return remote(ring_out.at[s, p], ring_in.at[s - 1, p], back_ring_s.at[n], back_ring_r.at[n - 2], before)
+        n = PIECES * s + p
+        return remote(
+            piece(ring_out.at[s], p), piece(ring_in.at[s - 1], p), back_ring_s.at[n], back_ring_r.at[n - PIECES], before
+        )
 
     def arrived(s, p):
-        n = 2 * s + p
-        return remote(ring_out.at[s, p], ring_in.at[s, p], back_ring_s.at[n], back_ring_r.at[n], before)
+        n = PIECES * s + p
+        return remote(piece(ring_out.at[s], p), piece(ring_in.at[s], p), back_ring_s.at[n], back_ring_r.at[n], before)
 
     def settle(s):
-        direct = DIAG and s == last
-        if not direct:
-            back_side(s).wait_recv()
-        if DIAG and s == last - 1:
-            back_diag().wait_recv()
-        for p in range(2):
-            whole = near[s, p]
-            if not direct:
-                whole = whole + pair_in[s, p].astype(F32)
-            if DIAG and s == last - 1:
-                whole = whole + diag_in[p].astype(F32)
+        back_side(s).wait_recv()
+        per = PIECES // 2
+        length = tokens // per
+        for p in range(PIECES):
+            at = (p // per, slice((p % per) * length, (p % per + 1) * length))
+            whole = near[(s, *at)] + pair_in[(s, *at)].astype(F32)
             if s < last:
                 arrived(s, p).wait_recv()
-                whole = whole + ring_in[s, p].astype(F32)
-            ring_out[s, p] = whole.astype(BF16)
+                whole = whole + ring_in[(s, *at)].astype(F32)
             if s > 0:
+                ring_out[(s, *at)] = whole.astype(BF16)
                 back_ring(s, p).start()
+            else:
+                (dk_ref, dv_ref)[at[0]][at[1], :] = whole.astype(BF16)
 
     def leave(n, _):
-        s = last - n
-        dk, dv = backward(2 * s + 1)
-        pair_out[s, 0] = dk.astype(BF16)
-        pair_out[s, 1] = dv.astype(BF16)
-        if DIAG:
-            @pl.when(n == 0)
-            def _():
-                back_diag().start()
-
-            @pl.when(n > 0)
-            def _():
-                back_side(s).start()
-        else:
+        s, j = last - 2 * (n // 4) - n % 2, 1 - (n % 4) // 2
+        dk, dv = backward(2 * s + j)
+
+        @pl.when(j == 1)
+        def _():
+            pair_out[s, 0] = dk.astype(BF16)
+            pair_out[s, 1] = dv.astype(BF16)
             back_side(s).start()
-        dk, dv = backward(2 * s)
-        near[s, 0] = dk
-        near[s, 1] = dv
-
-        @pl.when(n == (0 if DIAG else 2))
+
+        @pl.when(j == 0)
+        def _():
+            near[s, 0] = dk
+            near[s, 1] = dv
+
+        @pl.when(n == 5)
         def _():
             settle(last)
 
         return 0
 
-    lax.fori_loop(0, STEPS, leave, 0)
+    lax.fori_loop(0, 2 * STEPS, leave, 0)
 
     dq_over = remote(dq_cols.at[:, pl.ds(own_rows, own_rows)], dq_in, dq_s.at[0], dq_r.at[0], mate)
     dq_over.start()
@@ -281,34 +266,28 @@
     for h in range(heads):
         there = slice(h * tokens, (h + 1) * tokens)
         part = (dq_cols[:, there] + dq_in[:, there]) * scale
-        dq_rows[:, h * size : (h + 1) * size] = part.T.astype(BF16)
-    store_dq = pltpu.make_async_copy(dq_rows, dq_hbm, store_sem.at[0])
-    store_dq.start()
+        dq_ref[:, h * size : (h + 1) * size] = part.T.astype(BF16)
     for s in reversed(range(last - 1)):
         settle(s)
-    store_dk = pltpu.make_async_copy(ring_out.at[0, 0], dk_hbm, store_sem.at[1])
-    store_dv = pltpu.make_async_copy(ring_out.at[0, 1], dv_hbm, store_sem.at[2])
-    store_dk.start()
-    store_dv.start()
     q_over.wait_send()
     g_over.wait_send()
     dq_over.wait_send()
     for s in range(STEPS):
-        for p in range(2):
+        for p in range(PIECES):
             if s < last:
                 ring(s, p).wait_send()
                 back_ring(s + 1, p).wait_send()
-            if s < last or not DIAG:
-                side(s, p).wait_send()
-            if s == last and DIAG:
-                diag(p).wait_send()
-        if s < last or not DIAG:
-            back_side(s).wait_send()
-        else:
-            back_diag().wait_send()
-    store_dq.wait()
-    store_dk.wait()
-    store_dv.wait()
+            side(s, p).wait_send()
+        back_side(s).wait_send()
+
+
+def store(*refs):
+    sem, count = refs[-1], len(refs) // 2
+    copies = [pltpu.make_async_copy(refs[n], refs[count + n], sem.at[n]) for n in range(count)]
+    for copy in copies:
+        copy.start()
+    for copy in copies:
+        copy.wait()
 
 
 def per_device(queries, keys, values, out_grad, block_place):
@@ -324,15 +303,15 @@
     body = functools.partial(
         kernel, lax.axis_size("inner"), lax.axis_size("outer"), tokens, size, heads
     )
-    return pl.pallas_call(
+    results = pl.pallas_call(
         body,
         out_shape=(
-            jax.ShapeDtypeStruct(queries.shape, BF16),
-            jax.ShapeDtypeStruct(keys.shape, BF16),
-            jax.ShapeDtypeStruct(values.shape, BF16),
+            pltpu.VMEM(queries.shape, BF16),
+            pltpu.VMEM(keys.shape, BF16),
+            pltpu.VMEM(values.shape, BF16),
         ),
         in_specs=[pl.BlockSpec(memory_space=pltpu.SMEM), hbm, hbm, hbm, hbm],
-        out_specs=(hbm, hbm, hbm),
+        out_specs=(pl.BlockSpec(memory_space=pltpu.VMEM),) * 3,
         scratch_shapes=[
             low(chunks, 2, tokens, size),
             low(2, tokens, heads * size), low(2, tokens, heads * size), low(size, rows), low(size, rows),
@@ -340,11 +319,9 @@
             kept(8, rows), kept(8, rows), kept(size, rows), kept(size, own_rows),
             kept(STEPS, 2, tokens, size),
             low(STEPS, 2, tokens, size), low(STEPS, 2, tokens, size),
-            low(STEPS, 2, tokens, size), low(STEPS, 2, tokens, size), low(2, tokens, size),
-            low(tokens, heads * size),
-            dma(4), dma(3), dma(2), dma(2), dma(2), dma(2), dma(1), dma(1),
-            dma(chunks), dma(chunks), dma(chunks), dma(chunks), dma(2), dma(2),
-            dma(chunks), dma(chunks), dma(STEPS), dma(STEPS), dma(1), dma(1),
+            low(STEPS, 2, tokens, size), low(STEPS, 2, tokens, size),
+            dma(4), dma(2), dma(2), dma(2), dma(2), dma(1), dma(1),
+            *[dma(PIECES * STEPS)] * 6, dma(STEPS), dma(STEPS),
         ],
         compiler_params=pltpu.CompilerParams(
             collective_id=0, has_side_effects=True, vmem_limit_bytes=58 * 2**20
@@ -356,6 +333,15 @@
         ),
         name="attention_backward",
     )(block_place, queries, keys, values, out_grad)
+    shapes = tuple(jax.ShapeDtypeStruct(r.shape, r.dtype) for r in results)
+    return pl.pallas_call(
+        store,
+        out_shape=shapes,
+        in_specs=[pl.BlockSpec(memory_space=pltpu.VMEM)] * len(shapes),
+        out_specs=(hbm,) * len(shapes),
+        scratch_shapes=[dma(len(shapes))],
+        name="store_gradients",
+    )(*(pltpu.with_memory_space_constraint(r, pltpu.VMEM) for r in results))
 
 
 def solution(mesh):

time: 52.6 us -> 49.6 us (0.943)
  local copies, waits for them, and re-layouts: 3.2 us -> 0 us
    unnamed x7 -> x0, local copies, waits for them, and re-layouts: 3.2 us -> none
    pallas_call x1 -> x2, Pallas kernels: 48.6 us -> 48.9 us  [the longest x1 48.1 us: per_device(): pl.pallas_call(body, out_shape=(pltpu.VMEM(queries.shape, BF16), pltpu.VM...]
where the time goes in v3:
time: 49.6 us; the launch traced here: 49.5 us
  Pallas kernels  48.9 us (99%)
  between operations  0.64 us (1%)
    pallas_call x1, Pallas kernels, per_device(): pl.pallas_call(body, out_shape=(pltpu.VMEM(queries.shape, BF16), pltpu.VM...  48.1 us

profile of v3, /device:TPU:1, one launch (start us, length us, event | category | flops | bytes accessed | tf_op | source)
XLA Modules:
  0.0 49.5 jit_solution(13375027893646487278)
XLA Ops:
  0.6 48.1 %attention_backward.1 = (bf16[256,512]{1,0:T(8,128)(2,1)S(1)}, bf16[256,128]{1,0:T(8,128)(2,1)S(1)}, bf16[256,128]{1,0:T(8,128)(2,1)S(1)}) custom-call(s32[512]{0:T(512)} %place_ref.1, bf16[256,512]{1,0:T(8,128)(2,1)} %q_hbm.1, bf16[256,128]{1,0:T(8,128)(2,1)} %k_hbm.1, bf16[256,128]{1,0:T(8,128)(2,1)} %v_hbm.1, bf16[256,512]{1,0:T(8,128)(2,1)} %g_hbm.1), custom_call_target="tpu_custom_call" | custom-call | flops 5368709120 | bytes 983040 | tf_op jit(solution)/shard_map/attention_backward/pallas_call | solution.py:306
  48.8 0.8 %store_gradients.1 = (bf16[256,512]{1,0:T(8,128)(2,1)}, bf16[256,128]{1,0:T(8,128)(2,1)}, bf16[256,128]{1,0:T(8,128)(2,1)}) custom-call(bf16[256,512]{1,0:T(8,128)(2,1)S(1)} %get-tuple-element.6.refs_0_, bf16[256,128]{1,0:T(8,128)(2,1)S(1)} %get-tuple-element.7.refs_1_, bf16[256,128]{1,0:T(8,128)(2,1)S(1)} %get-tuple-element.8.refs_2_), custom_call_target="tpu_custom_call" | custom-call | tf_op jit(solution)/shard_map/store_gradients/pallas_call | solution.py:337

commit v4 on v3

--- a/solution.py
+++ b/solution.py
@@ -48,7 +48,7 @@
     loads = [
         pltpu.make_async_copy(src, dst, load_sem.at[n])
         for n, (src, dst) in enumerate(
-            ((k_hbm, kv.at[0, 0]), (v_hbm, kv.at[0, 1]), (q_hbm, q_nat.at[0]), (g_hbm, g_nat.at[0]))
+            ((k_hbm, kv.at[0, 0]), (v_hbm, kv.at[0, 1]), (q_hbm, q_nat.at[core]), (g_hbm, g_nat.at[core]))
         )
     ]
     for load in loads:
@@ -78,8 +78,8 @@
         n = PIECES * s + p
         return remote(piece(kv.at[2 * s], p), piece(kv.at[2 * s + 1], p), pair_s.at[n], pair_r.at[n], pair)
 
-    q_over = remote(q_hbm, q_nat.at[1], q_s.at[0], q_r.at[0], mate)
-    g_over = remote(g_hbm, g_nat.at[1], q_s.at[1], q_r.at[1], mate)
+    q_over = remote(q_hbm, q_nat.at[core], q_s.at[0], q_r.at[0], mate)
+    g_over = remote(g_hbm, g_nat.at[core], q_s.at[1], q_r.at[1], mate)
     loads[0].wait()
     loads[1].wait()
     for p in range(PIECES):
@@ -95,35 +95,35 @@
         first_block = 2 * (side_inner * outer_size + outer)
         return jnp.where((lane // block) % 2 == 0, place_ref[first_block], place_ref[first_block + 1])
 
-    q_place = jnp.concatenate([row_places(inner), row_places(other_core)], axis=1)
+    q_place = jnp.concatenate([row_places(inner - core), row_places(inner - core + 1)], axis=1)
 
     def turn(n):
         for h in range(heads):
-            there = pl.ds(n * own_rows + h * tokens, tokens)
+            there = pl.ds(pl.multiple_of(n * own_rows + h * tokens, tokens), tokens)
             q_cols[:, there] = q_nat[n, :, h * size : (h + 1) * size].T
             g_cols[:, there] = g_nat[n, :, h * size : (h + 1) * size].T
 
     loads[2].wait()
     loads[3].wait()
-    turn(0)
+    turn(core)
     q_over.wait_recv()
     g_over.wait_recv()
-    turn(1)
+    turn(1 - core)
 
     def key_block(s, j):
         crossed = jnp.where(depth < s, core, 0)
         column = (inner + 2 * crossed + 2 * j) % inner_size
         return 2 * (column * outer_size + (outer + outer_size - s) % outer_size)
 
-    def forward(s, j, first=False):
+    def forward(s, j, first=False, tiles=range(rows // tokens)):
         c = 2 * s + j
         keys, values = kv[c, 0], kv[c, 1]
         places = [place_ref[key_block(s, j) + b] for b in range(2)]
-        for t in range(rows // tokens):
+        for t in tiles:
             at = slice(t * tokens, (t + 1) * tokens)
             place = q_place[:, at]
             bias = [jnp.broadcast_to(jnp.where(p <= place, 0.0, LOW).astype(F32), (block, tokens)) for p in places]
-            if first and t < heads:
+            if first:
                 row = lax.broadcasted_iota(jnp.int32, (block, tokens), 0)
                 col = lax.broadcasted_iota(jnp.int32, (block, tokens), 1) % block
                 for b in range(2):
@@ -171,41 +171,43 @@
     last = STEPS - 1
     for p in range(PIECES):
         side(last, p).wait_recv()
-    forward(last, 1)
-
-    def swap_stats(n):
-        here = pl.ds(n * own_rows, own_rows)
-        there = pl.ds((1 - n) * own_rows, own_rows)
-        return remote(stats.at[:, here], stats_in.at[:, there], stats_s.at[n], stats_r.at[n], mate)
-
+    dq_cols[...] = jnp.zeros_like(dq_cols)
+
+    def join(n):
+        at = pl.ds(n * own_rows, own_rows)
+        return remote(stats.at[:, at], stats_in.at[:, at], stats_s.at[n], stats_r.at[n], mate)
+
+    def joined(n):
+        join(n).wait()
+        at = slice(n * own_rows, (n + 1) * own_rows)
+        top = jnp.maximum(stats[0:1, at], stats_in[0:1, at])
+        here, there = jnp.exp2(stats[0:1, at] - top), jnp.exp2(stats_in[0:1, at] - top)
+        inverse = 1.0 / (stats[1:2, at] * here + stats_in[1:2, at] * there)
+        mean = (stats[2:3, at] * here + stats_in[2:3, at] * there) * inverse
+        stats[0:1, at] = top
+        stats[1:2, at] = inverse
+        stats[2:3, at] = mean
+
+    halves = [range(n * heads, (n + 1) * heads) for n in range(2)]
     for n in range(2):
-        swap_stats(n).start()
-    dq_cols[...] = jnp.zeros_like(dq_cols)
-    for n in range(2):
-        swap_stats(n).wait()
-    top = jnp.maximum(stats[0:1, :], stats_in[0:1, :])
-    here, there = jnp.exp2(stats[0:1, :] - top), jnp.exp2(stats_in[0:1, :] - top)
-    inverse = 1.0 / (stats[1:2, :] * here + stats_in[1:2, :] * there)
-    mean = (stats[2:3, :] * here + stats_in[2:3, :] * there) * inverse
-    stats[0:1, :] = top
-    stats[1:2, :] = inverse
-    stats[2:3, :] = mean
-
-    def backward(c):
+        forward(last, 1, tiles=halves[n])
+        join(n).start()
+
+    def backward(c, tiles=range(rows // tokens), dk=None, dv=None):
         keys = kv[c, 0]
-        dk = jnp.zeros((tokens, size), F32)
-        dv = jnp.zeros((tokens, size), F32)
-        factor = jnp.exp2(maxes[c] - stats[0:1, :]) * stats[1:2, :]
-        for t in range(rows // tokens):
+        dk = jnp.zeros((tokens, size), F32) if dk is None else dk
+        dv = jnp.zeros((tokens, size), F32) if dv is None else dv
+        for t in tiles:
             at = slice(t * tokens, (t + 1) * tokens)
             n, h = t // heads, t % heads
             cut = slice(h * size, (h + 1) * size)
-            weights = probs[c, :, at].astype(F32) * factor[:, at]
+            factor = jnp.exp2(maxes[c, :, at] - stats[0:1, at]) * stats[1:2, at]
+            weights = probs[c, :, at].astype(F32) * factor
             slopes = (weights * (grads[c, :, at] - stats[2:3, at])).astype(BF16)
             dv += dot(weights.astype(BF16), g_nat[n, :, cut])
             dk += dot(slopes, q_nat[n, :, cut])
             dq_cols[:, at] += dot(keys, slopes, (0, 0))
-        return dk * scale, dv
+        return dk, dv
 
     def back_side(s):
         return remote(pair_out.at[s], pair_in.at[s], back_pair_s.at[s], back_pair_r.at[s], pair)
@@ -236,9 +238,18 @@
             else:
                 (dk_ref, dv_ref)[at[0]][at[1], :] = whole.astype(BF16)
 
+    joined(0)
+    dk, dv = backward(2 * last + 1, halves[0])
+    joined(1)
+    dk, dv = backward(2 * last + 1, halves[1], dk, dv)
+    pair_out[last, 0] = (dk * scale).astype(BF16)
+    pair_out[last, 1] = dv.astype(BF16)
+    back_side(last).start()
+
     def leave(n, _):
-        s, j = last - 2 * (n // 4) - n % 2, 1 - (n % 4) // 2
+        s, j = last - n // 2, 1 - n % 2
         dk, dv = backward(2 * s + j)
+        dk = dk * scale
 
         @pl.when(j == 1)
         def _():
@@ -251,21 +262,21 @@
             near[s, 0] = dk
             near[s, 1] = dv
 
-        @pl.when(n == 5)
+        @pl.when(n == 4)
         def _():
             settle(last)
 
         return 0
 
-    lax.fori_loop(0, 2 * STEPS, leave, 0)
-
-    dq_over = remote(dq_cols.at[:, pl.ds(own_rows, own_rows)], dq_in, dq_s.at[0], dq_r.at[0], mate)
+    lax.fori_loop(1, 2 * STEPS, leave, 0)
+
+    dq_over = remote(dq_cols.at[:, pl.ds(pl.multiple_of((1 - core) * own_rows, own_rows), own_rows)], dq_in, dq_s.at[0], dq_r.at[0], mate)
     dq_over.start()
     settle(last - 1)
     dq_over.wait_recv()
     for h in range(heads):
-        there = slice(h * tokens, (h + 1) * tokens)
-        part = (dq_cols[:, there] + dq_in[:, there]) * scale
+        here = pl.ds(pl.multiple_of(core * own_rows + h * tokens, tokens), tokens)
+        part = (dq_cols[:, here] + dq_in[:, h * tokens : (h + 1) * tokens]) * scale
         dq_ref[:, h * size : (h + 1) * size] = part.T.astype(BF16)
     for s in reversed(range(last - 1)):
         settle(s)

time: 49.6 us -> 49.2 us (level)
  no operation moved by 1% of the time
where the time goes in v4:
time: 49.2 us; the launch traced here: 49.1 us
  Pallas kernels  48.5 us (99%)
  between operations  0.64 us (1%)
    pallas_call x1, Pallas kernels, per_device(): pl.pallas_call(body, out_shape=(pltpu.VMEM(queries.shape, BF16), pltpu.VM...  47.7 us

profile of v4, /device:TPU:1, one launch (start us, length us, event | category | flops | bytes accessed | tf_op | source)
XLA Modules:
  0.0 49.1 jit_solution(2755020794389349035)
XLA Ops:
  0.6 47.7 %attention_backward.1 = (bf16[256,512]{1,0:T(8,128)(2,1)S(1)}, bf16[256,128]{1,0:T(8,128)(2,1)S(1)}, bf16[256,128]{1,0:T(8,128)(2,1)S(1)}) custom-call(s32[512]{0:T(512)} %place_ref.1, bf16[256,512]{1,0:T(8,128)(2,1)} %q_hbm.1, bf16[256,128]{1,0:T(8,128)(2,1)} %k_hbm.1, bf16[256,128]{1,0:T(8,128)(2,1)} %v_hbm.1, bf16[256,512]{1,0:T(8,128)(2,1)} %g_hbm.1), custom_call_target="tpu_custom_call" | custom-call | flops 5368709120 | bytes 983040 | tf_op jit(solution)/shard_map/attention_backward/pallas_call | solution.py:317
  48.3 0.8 %store_gradients.1 = (bf16[256,512]{1,0:T(8,128)(2,1)}, bf16[256,128]{1,0:T(8,128)(2,1)}, bf16[256,128]{1,0:T(8,128)(2,1)}) custom-call(bf16[256,512]{1,0:T(8,128)(2,1)S(1)} %get-tuple-element.6.refs_0_, bf16[256,128]{1,0:T(8,128)(2,1)S(1)} %get-tuple-element.7.refs_1_, bf16[256,128]{1,0:T(8,128)(2,1)S(1)} %get-tuple-element.8.refs_2_), custom_call_target="tpu_custom_call" | custom-call | tf_op jit(solution)/shard_map/store_gradients/pallas_call | solution.py:348

commit v5 on v4

--- a/solution.py
+++ b/solution.py
@@ -273,13 +273,13 @@
     dq_over = remote(dq_cols.at[:, pl.ds(pl.multiple_of((1 - core) * own_rows, own_rows), own_rows)], dq_in, dq_s.at[0], dq_r.at[0], mate)
     dq_over.start()
     settle(last - 1)
+    settle(1)
     dq_over.wait_recv()
     for h in range(heads):
         here = pl.ds(pl.multiple_of(core * own_rows + h * tokens, tokens), tokens)
         part = (dq_cols[:, here] + dq_in[:, h * tokens : (h + 1) * tokens]) * scale
         dq_ref[:, h * size : (h + 1) * size] = part.T.astype(BF16)
-    for s in reversed(range(last - 1)):
-        settle(s)
+    settle(0)
     q_over.wait_send()
     g_over.wait_send()
     dq_over.wait_send()

time: 49.2 us -> 49.2 us (level)
  no operation moved by 1% of the time
where the time goes in v5:
time: 49.2 us; the launch traced here: 49.1 us
  Pallas kernels  48.5 us (99%)
  between operations  0.64 us (1%)
    pallas_call x1, Pallas kernels, per_device(): pl.pallas_call(body, out_shape=(pltpu.VMEM(queries.shape, BF16), pltpu.VM...  47.7 us

profile of v5, /device:TPU:1, one launch (start us, length us, event | category | flops | bytes accessed | tf_op | source)
XLA Modules:
  0.0 49.1 jit_solution(12446744145775071022)
XLA Ops:
  0.6 47.7 %attention_backward.1 = (bf16[256,512]{1,0:T(8,128)(2,1)S(1)}, bf16[256,128]{1,0:T(8,128)(2,1)S(1)}, bf16[256,128]{1,0:T(8,128)(2,1)S(1)}) custom-call(s32[512]{0:T(512)} %place_ref.1, bf16[256,512]{1,0:T(8,128)(2,1)} %q_hbm.1, bf16[256,128]{1,0:T(8,128)(2,1)} %k_hbm.1, bf16[256,128]{1,0:T(8,128)(2,1)} %v_hbm.1, bf16[256,512]{1,0:T(8,128)(2,1)} %g_hbm.1), custom_call_target="tpu_custom_call" | custom-call | flops 5368709120 | bytes 983040 | tf_op jit(solution)/shard_map/attention_backward/pallas_call | solution.py:317
  48.3 0.8 %store_gradients.1 = (bf16[256,512]{1,0:T(8,128)(2,1)}, bf16[256,128]{1,0:T(8,128)(2,1)}, bf16[256,128]{1,0:T(8,128)(2,1)}) custom-call(bf16[256,512]{1,0:T(8,128)(2,1)S(1)} %get-tuple-element.6.refs_0_, bf16[256,128]{1,0:T(8,128)(2,1)S(1)} %get-tuple-element.7.refs_1_, bf16[256,128]{1,0:T(8,128)(2,1)S(1)} %get-tuple-element.8.refs_2_), custom_call_target="tpu_custom_call" | custom-call | tf_op jit(solution)/shard_map/store_gradients/pallas_call | solution.py:348
